TPU v7x, 256 devices: a whole 4x4x8 slice. The times are simulated.
256 devices in a mesh: head: 8 (over x, z_lo), blk: 32 (over y, z_hi, core).
Axes of the slice: x: 4, y: 4, z: 8 (z_hi: 4, z_lo: 2; z = z_hi * 2 + z_lo), core: 2. Of those that a mesh axis runs over, the one named last changes fastest.
Arguments:
- queries: bfloat16 [8192, 3072], P(('blk', 'head')), may hold values from -6 to 6
- key_rows: bfloat16 [8192, 3072], P(('blk', 'head')), may hold values from -6 to 6
- values: bfloat16 [8192, 3072], P(('blk', 'head')), may hold values from -4 to 4
- tile_mask: int32 [64, 64], replicated, may hold values from 0 to 1, as said below
Outputs:
- attended: float32 [8192, 3072], P(('blk', 'head'))
Inputs may be any that keep to these rules, and one draw needn't show every extreme that they name: tile_mask[i, j] is 1 exactly when key tile j lies within query tile i's 3-D window; tile i sits at time level i // 16, row (i // 4) % 4 and column i % 4 of a grid of 4 x 4 x 4 tiles; each time level of query tiles has its own window, whose backward and forward half-widths along each of the three directions are 1 or 2 tiles, drawn separately.
All inputs are finite; a program needn't handle non-finite values.
Results may differ from a plain program's by a relative error of at most 0.0025.
Values may be sent and summed in bfloat16 or wider, within the bound.
A program may use at most 128 MiB of HBM per device.

v0:
```python
import jax
import jax.numpy as jnp
from jax import lax
from jax.sharding import PartitionSpec as P

HEAD_DIM = 128
TILE = 128


masked_level = -1e30


def passed_along(block, axis, distance):
    devices = range(lax.axis_size(axis))
    route = [((i - distance) % len(devices), i) for i in devices]
    return lax.ppermute(block, axis, route)


def expand_tiles(tile_block, tile):
    tile_count = tile_block.shape[0]
    spread = jnp.broadcast_to(
        tile_block[:, None, :, None] > 0, (tile_count, tile, tile_count, tile)
    )
    return spread.reshape(tile_count * tile, tile_count * tile)


def block_partial(query_block, key_block, value_block, allowed):
    score_scale = query_block.shape[-1] ** (-0.5)
    scores = (
        jnp.einsum("qhd,khd->hqk", query_block, key_block, preferred_element_type=jnp.float32)
        * score_scale
    )
    masked = jnp.where(allowed[None], scores, masked_level)
    row_peak = jnp.max(masked, axis=-1)
    weights = jnp.where(allowed[None], jnp.exp(masked - row_peak[..., None]), 0.0)
    totals = jnp.sum(weights, axis=-1)
    rounded = weights.astype(jnp.bfloat16)
    mixture = jnp.einsum("hqk,khd->qhd", rounded, value_block, preferred_element_type=jnp.float32)
    safe_totals = jnp.maximum(totals, 1.0)
    partial_value = mixture / safe_totals.T[:, :, None]
    partial_lse = jnp.where(totals > 0, row_peak + jnp.log(safe_totals), masked_level)
    return (partial_value, partial_lse)


def combine_states(output, log_sums, partial_value, partial_lse):
    highest = jnp.maximum(log_sums, partial_lse)
    combined = highest + jnp.log(jnp.exp(log_sums - highest) + jnp.exp(partial_lse - highest))
    mixed_out = (
        output * jnp.exp(log_sums - combined).T[:, :, None]
        + partial_value * jnp.exp(partial_lse - combined).T[:, :, None]
    )
    return (mixed_out, combined)


def visit_block(
    carried_state, query_block, key_block, value_block, tile_mask, query_slab, key_slab
):
    tile_count = query_block.shape[0] // TILE
    tile_block = lax.dynamic_slice(
        tile_mask, (query_slab * tile_count, key_slab * tile_count), (tile_count, tile_count)
    )

    def include(state_pair):
        partial_value, partial_lse = block_partial(
            query_block, key_block, value_block, expand_tiles(tile_block, TILE)
        )
        return combine_states(state_pair[0], state_pair[1], partial_value, partial_lse)

    def unchanged(state_pair):
        return state_pair

    return lax.cond(jnp.any(tile_block > 0), include, unchanged, carried_state)


def local(queries, key_rows, values, tile_mask):
    query_part, key_part, value_part = (
        lax.all_to_all(queries, "head", split_axis=1, concat_axis=0, tiled=True),
        lax.all_to_all(key_rows, "head", split_axis=1, concat_axis=0, tiled=True),
        lax.all_to_all(values, "head", split_axis=1, concat_axis=0, tiled=True),
    )
    slab_rows = query_part.shape[0]
    query_block = query_part.reshape(slab_rows, -1, HEAD_DIM)
    key_block = key_part.reshape(slab_rows, -1, HEAD_DIM)
    value_block = value_part.reshape(slab_rows, -1, HEAD_DIM)
    heads_local = query_block.shape[1]
    cycle_size = lax.axis_size("blk")
    own_index = lax.axis_index("blk")
    initial = (
        jnp.zeros((slab_rows, heads_local, HEAD_DIM), jnp.float32),
        jnp.full((heads_local, slab_rows), masked_level, jnp.float32),
    )

    def cycle_turn(offset, carried):
        moving, output, log_sums = carried
        query_slab = (own_index - offset) % cycle_size
        output, log_sums = visit_block(
            (output, log_sums), moving, key_block, value_block, tile_mask, query_slab, own_index
        )
        shifted = passed_along((moving.astype(jnp.float32), output, log_sums), "blk", 1)
        return (shifted[0].astype(jnp.bfloat16), shifted[1], shifted[2])

    moving, output, log_sums = lax.fori_loop(
        0, cycle_size - 1, cycle_turn, (query_block, initial[0], initial[1])
    )
    output, log_sums = visit_block(
        (output, log_sums),
        moving,
        key_block,
        value_block,
        tile_mask,
        (own_index + 1) % cycle_size,
        own_index,
    )
    returned = passed_along((output, log_sums), "blk", 1)
    output = returned[0]
    attended = output.reshape(slab_rows, -1)
    return lax.all_to_all(attended, "head", split_axis=0, concat_axis=1, tiled=True)


def solution(mesh):
    return jax.shard_map(
        local,
        mesh=mesh,
        in_specs=(
            P(("blk", "head"), None),
            P(("blk", "head"), None),
            P(("blk", "head"), None),
            P(),
        ),
        out_specs=P(("blk", "head"), None),
        check_vma=False,
    )
```

profile of v0, /device:TPU:16, one launch (start us, length us, event | category | flops | bytes accessed | tf_op | source)
XLA Modules:
  0.0 691.6 jit_solution(2683086782463851970)
XLA Ops:
  1.6 5.8 all-to-all-start.1
  8.1 6.3 all-to-all-done.1
  14.4 3.5 all-to-all-start.2
  18.6 6.2 all-to-all-done.2
  24.8 3.4 all-to-all-start
  30.5 4.6 all-to-all-done
  35.2 623.3 %while.22 = (s32[]{:T(128)}, bf16[256,3,128]{2,0,1:T(8,128)(2,1)S(1)}, f32[256,3,128]{2,0,1:T(8,128)S(1)}, f32[3,256]{1,0:T(4,128)S(1)}, s32[]{:T(128)}, /*index...) while((s32[]{:T(128)}, ...), condition=%wide.region_7.8_spmd, body=%wide.region_1.7_spmd.sunk | while | flops 102835992 | bytes 7870026 | solution.py:102
  39.1 3.4 collective-permute-start
  42.5 11.5 %collective-permute-done.2 = f32[3,256]{1,0:T(4,128)S(1)} collective-permute-done((f32[3,256]{1,0:T(4,128)S(1)}, f32[3,256]{1,0:T(4,128)S(1)}, u32[]{:S(2)}, u32[]{:S(2)}) %collective-permute-start.2) | collective-permute-done | bytes 3104 | tf_op jit(solution)/shard_map/while/body/eval_jaxpr/ppermute | solution.py:16
  56.3 3.3 collective-permute-start
  59.6 2.3 collective-permute-start.2
  61.9 6.9 %collective-permute-done.2 = f32[3,256]{1,0:T(4,128)S(1)} collective-permute-done((f32[3,256]{1,0:T(4,128)S(1)}, f32[3,256]{1,0:T(4,128)S(1)}, u32[]{:S(2)}, u32[]{:S(2)}) %collective-permute-start.2) | collective-permute-done | bytes 3104 | tf_op jit(solution)/shard_map/while/body/eval_jaxpr/ppermute | solution.py:16
  71.1 3.4 collective-permute-start
  74.5 9.1 %collective-permute-start.2 = (f32[3,256]{1,0:T(4,128)S(1)}, f32[3,256]{1,0:T(4,128)S(1)}, u32[]{:S(2)}, u32[]{:S(2)}) collective-permute-start(f32[3,256]{1,0:T(4,128)S(1)} %get-tuple-element.397), channel_id=1, source_target_pairs={{31,0},{0,1},{1,2},{2,3},{3,4},{4,5},{5,6},{6,7},{7,8},{8,9},{9,10... | collective-permute-start | bytes 9224 | tf_op jit(solution)/shard_map/while/body/eval_jaxpr/ppermute | solution.py:16
  88.2 5.6 collective-permute-start.1
  93.8 5.0 collective-permute-start
  100.1 8.2 %collective-permute-done.2 = f32[3,256]{1,0:T(4,128)S(1)} collective-permute-done((f32[3,256]{1,0:T(4,128)S(1)}, f32[3,256]{1,0:T(4,128)S(1)}, u32[]{:S(2)}, u32[]{:S(2)}) %collective-permute-start.2) | collective-permute-done | bytes 3104 | tf_op jit(solution)/shard_map/while/body/eval_jaxpr/ppermute | solution.py:16
  112.1 3.8 collective-permute-start.1
  115.9 3.4 collective-permute-start
  119.4 11.5 %collective-permute-done.2 = f32[3,256]{1,0:T(4,128)S(1)} collective-permute-done((f32[3,256]{1,0:T(4,128)S(1)}, f32[3,256]{1,0:T(4,128)S(1)}, u32[]{:S(2)}, u32[]{:S(2)}) %collective-permute-start.2) | collective-permute-done | bytes 3104 | tf_op jit(solution)/shard_map/while/body/eval_jaxpr/ppermute | solution.py:16
  135.0 16.0 %collective-permute-done.2 = f32[3,256]{1,0:T(4,128)S(1)} collective-permute-done((f32[3,256]{1,0:T(4,128)S(1)}, f32[3,256]{1,0:T(4,128)S(1)}, u32[]{:S(2)}, u32[]{:S(2)}) %collective-permute-start.2) | collective-permute-done | bytes 3104 | tf_op jit(solution)/shard_map/while/body/eval_jaxpr/ppermute | solution.py:16
  155.1 14.8 %collective-permute-done.2 = f32[3,256]{1,0:T(4,128)S(1)} collective-permute-done((f32[3,256]{1,0:T(4,128)S(1)}, f32[3,256]{1,0:T(4,128)S(1)}, u32[]{:S(2)}, u32[]{:S(2)}) %collective-permute-start.2) | collective-permute-done | bytes 3104 | tf_op jit(solution)/shard_map/while/body/eval_jaxpr/ppermute | solution.py:16
  174.0 17.5 %collective-permute-done.2 = f32[3,256]{1,0:T(4,128)S(1)} collective-permute-done((f32[3,256]{1,0:T(4,128)S(1)}, f32[3,256]{1,0:T(4,128)S(1)}, u32[]{:S(2)}, u32[]{:S(2)}) %collective-permute-start.2) | collective-permute-done | bytes 3104 | tf_op jit(solution)/shard_map/while/body/eval_jaxpr/ppermute | solution.py:16
  195.6 15.0 %collective-permute-done.2 = f32[3,256]{1,0:T(4,128)S(1)} collective-permute-done((f32[3,256]{1,0:T(4,128)S(1)}, f32[3,256]{1,0:T(4,128)S(1)}, u32[]{:S(2)}, u32[]{:S(2)}) %collective-permute-start.2) | collective-permute-done | bytes 3104 | tf_op jit(solution)/shard_map/while/body/eval_jaxpr/ppermute | solution.py:16
  213.0 18.4 %collective-permute-done.2 = f32[3,256]{1,0:T(4,128)S(1)} collective-permute-done((f32[3,256]{1,0:T(4,128)S(1)}, f32[3,256]{1,0:T(4,128)S(1)}, u32[]{:S(2)}, u32[]{:S(2)}) %collective-permute-start.2) | collective-permute-done | bytes 3104 | tf_op jit(solution)/shard_map/while/body/eval_jaxpr/ppermute | solution.py:16
  233.9 18.5 %collective-permute-done.2 = f32[3,256]{1,0:T(4,128)S(1)} collective-permute-done((f32[3,256]{1,0:T(4,128)S(1)}, f32[3,256]{1,0:T(4,128)S(1)}, u32[]{:S(2)}, u32[]{:S(2)}) %collective-permute-start.2) | collective-permute-done | bytes 3104 | tf_op jit(solution)/shard_map/while/body/eval_jaxpr/ppermute | solution.py:16
  254.9 17.7 %collective-permute-done.2 = f32[3,256]{1,0:T(4,128)S(1)} collective-permute-done((f32[3,256]{1,0:T(4,128)S(1)}, f32[3,256]{1,0:T(4,128)S(1)}, u32[]{:S(2)}, u32[]{:S(2)}) %collective-permute-start.2) | collective-permute-done | bytes 3104 | tf_op jit(solution)/shard_map/while/body/eval_jaxpr/ppermute | solution.py:16
  275.1 18.4 %collective-permute-done.2 = f32[3,256]{1,0:T(4,128)S(1)} collective-permute-done((f32[3,256]{1,0:T(4,128)S(1)}, f32[3,256]{1,0:T(4,128)S(1)}, u32[]{:S(2)}, u32[]{:S(2)}) %collective-permute-start.2) | collective-permute-done | bytes 3104 | tf_op jit(solution)/shard_map/while/body/eval_jaxpr/ppermute | solution.py:16
  296.0 16.5 %collective-permute-done.2 = f32[3,256]{1,0:T(4,128)S(1)} collective-permute-done((f32[3,256]{1,0:T(4,128)S(1)}, f32[3,256]{1,0:T(4,128)S(1)}, u32[]{:S(2)}, u32[]{:S(2)}) %collective-permute-start.2) | collective-permute-done | bytes 3104 | tf_op jit(solution)/shard_map/while/body/eval_jaxpr/ppermute | solution.py:16
  314.9 18.5 %collective-permute-done.2 = f32[3,256]{1,0:T(4,128)S(1)} collective-permute-done((f32[3,256]{1,0:T(4,128)S(1)}, f32[3,256]{1,0:T(4,128)S(1)}, u32[]{:S(2)}, u32[]{:S(2)}) %collective-permute-start.2) | collective-permute-done | bytes 3104 | tf_op jit(solution)/shard_map/while/body/eval_jaxpr/ppermute | solution.py:16
  335.8 17.7 %collective-permute-done.2 = f32[3,256]{1,0:T(4,128)S(1)} collective-permute-done((f32[3,256]{1,0:T(4,128)S(1)}, f32[3,256]{1,0:T(4,128)S(1)}, u32[]{:S(2)}, u32[]{:S(2)}) %collective-permute-start.2) | collective-permute-done | bytes 3104 | tf_op jit(solution)/shard_map/while/body/eval_jaxpr/ppermute | solution.py:16
  356.0 17.3 %collective-permute-done.2 = f32[3,256]{1,0:T(4,128)S(1)} collective-permute-done((f32[3,256]{1,0:T(4,128)S(1)}, f32[3,256]{1,0:T(4,128)S(1)}, u32[]{:S(2)}, u32[]{:S(2)}) %collective-permute-start.2) | collective-permute-done | bytes 3104 | tf_op jit(solution)/shard_map/while/body/eval_jaxpr/ppermute | solution.py:16
  375.8 18.4 %collective-permute-done.2 = f32[3,256]{1,0:T(4,128)S(1)} collective-permute-done((f32[3,256]{1,0:T(4,128)S(1)}, f32[3,256]{1,0:T(4,128)S(1)}, u32[]{:S(2)}, u32[]{:S(2)}) %collective-permute-start.2) | collective-permute-done | bytes 3104 | tf_op jit(solution)/shard_map/while/body/eval_jaxpr/ppermute | solution.py:16
  396.6 18.0 %collective-permute-done.2 = f32[3,256]{1,0:T(4,128)S(1)} collective-permute-done((f32[3,256]{1,0:T(4,128)S(1)}, f32[3,256]{1,0:T(4,128)S(1)}, u32[]{:S(2)}, u32[]{:S(2)}) %collective-permute-start.2) | collective-permute-done | bytes 3104 | tf_op jit(solution)/shard_map/while/body/eval_jaxpr/ppermute | solution.py:16
  418.6 16.7 %collective-permute-done.2 = f32[3,256]{1,0:T(4,128)S(1)} collective-permute-done((f32[3,256]{1,0:T(4,128)S(1)}, f32[3,256]{1,0:T(4,128)S(1)}, u32[]{:S(2)}, u32[]{:S(2)}) %collective-permute-start.2) | collective-permute-done | bytes 3104 | tf_op jit(solution)/shard_map/while/body/eval_jaxpr/ppermute | solution.py:16
  439.4 14.4 %collective-permute-done.2 = f32[3,256]{1,0:T(4,128)S(1)} collective-permute-done((f32[3,256]{1,0:T(4,128)S(1)}, f32[3,256]{1,0:T(4,128)S(1)}, u32[]{:S(2)}, u32[]{:S(2)}) %collective-permute-start.2) | collective-permute-done | bytes 3104 | tf_op jit(solution)/shard_map/while/body/eval_jaxpr/ppermute | solution.py:16
  457.9 17.5 %collective-permute-done.2 = f32[3,256]{1,0:T(4,128)S(1)} collective-permute-done((f32[3,256]{1,0:T(4,128)S(1)}, f32[3,256]{1,0:T(4,128)S(1)}, u32[]{:S(2)}, u32[]{:S(2)}) %collective-permute-start.2) | collective-permute-done | bytes 3104 | tf_op jit(solution)/shard_map/while/body/eval_jaxpr/ppermute | solution.py:16
  479.4 17.4 %collective-permute-done.2 = f32[3,256]{1,0:T(4,128)S(1)} collective-permute-done((f32[3,256]{1,0:T(4,128)S(1)}, f32[3,256]{1,0:T(4,128)S(1)}, u32[]{:S(2)}, u32[]{:S(2)}) %collective-permute-start.2) | collective-permute-done | bytes 3104 | tf_op jit(solution)/shard_map/while/body/eval_jaxpr/ppermute | solution.py:16
  500.9 15.4 %collective-permute-done.2 = f32[3,256]{1,0:T(4,128)S(1)} collective-permute-done((f32[3,256]{1,0:T(4,128)S(1)}, f32[3,256]{1,0:T(4,128)S(1)}, u32[]{:S(2)}, u32[]{:S(2)}) %collective-permute-start.2) | collective-permute-done | bytes 3104 | tf_op jit(solution)/shard_map/while/body/eval_jaxpr/ppermute | solution.py:16
  520.4 15.0 %collective-permute-done.2 = f32[3,256]{1,0:T(4,128)S(1)} collective-permute-done((f32[3,256]{1,0:T(4,128)S(1)}, f32[3,256]{1,0:T(4,128)S(1)}, u32[]{:S(2)}, u32[]{:S(2)}) %collective-permute-start.2) | collective-permute-done | bytes 3104 | tf_op jit(solution)/shard_map/while/body/eval_jaxpr/ppermute | solution.py:16
  537.9 17.8 %collective-permute-done.2 = f32[3,256]{1,0:T(4,128)S(1)} collective-permute-done((f32[3,256]{1,0:T(4,128)S(1)}, f32[3,256]{1,0:T(4,128)S(1)}, u32[]{:S(2)}, u32[]{:S(2)}) %collective-permute-start.2) | collective-permute-done | bytes 3104 | tf_op jit(solution)/shard_map/while/body/eval_jaxpr/ppermute | solution.py:16
  558.2 18.4 %collective-permute-done.2 = f32[3,256]{1,0:T(4,128)S(1)} collective-permute-done((f32[3,256]{1,0:T(4,128)S(1)}, f32[3,256]{1,0:T(4,128)S(1)}, u32[]{:S(2)}, u32[]{:S(2)}) %collective-permute-start.2) | collective-permute-done | bytes 3104 | tf_op jit(solution)/shard_map/while/body/eval_jaxpr/ppermute | solution.py:16
  580.6 14.7 %collective-permute-done.2 = f32[3,256]{1,0:T(4,128)S(1)} collective-permute-done((f32[3,256]{1,0:T(4,128)S(1)}, f32[3,256]{1,0:T(4,128)S(1)}, u32[]{:S(2)}, u32[]{:S(2)}) %collective-permute-start.2) | collective-permute-done | bytes 3104 | tf_op jit(solution)/shard_map/while/body/eval_jaxpr/ppermute | solution.py:16
  599.4 16.0 %collective-permute-done.2 = f32[3,256]{1,0:T(4,128)S(1)} collective-permute-done((f32[3,256]{1,0:T(4,128)S(1)}, f32[3,256]{1,0:T(4,128)S(1)}, u32[]{:S(2)}, u32[]{:S(2)}) %collective-permute-start.2) | collective-permute-done | bytes 3104 | tf_op jit(solution)/shard_map/while/body/eval_jaxpr/ppermute | solution.py:16
  619.5 16.8 %collective-permute-done.2 = f32[3,256]{1,0:T(4,128)S(1)} collective-permute-done((f32[3,256]{1,0:T(4,128)S(1)}, f32[3,256]{1,0:T(4,128)S(1)}, u32[]{:S(2)}, u32[]{:S(2)}) %collective-permute-start.2) | collective-permute-done | bytes 3104 | tf_op jit(solution)/shard_map/while/body/eval_jaxpr/ppermute | solution.py:16
  640.4 18.1 %collective-permute-done.2 = f32[3,256]{1,0:T(4,128)S(1)} collective-permute-done((f32[3,256]{1,0:T(4,128)S(1)}, f32[3,256]{1,0:T(4,128)S(1)}, u32[]{:S(2)}, u32[]{:S(2)}) %collective-permute-start.2) | collective-permute-done | bytes 3104 | tf_op jit(solution)/shard_map/while/body/eval_jaxpr/ppermute | solution.py:16
  660.1 12.3 %collective-permute-done.3 = f32[256,3,128]{2,0,1:T(8,128)S(1)} collective-permute-done((f32[256,3,128]{2,0,1:T(8,128)S(1)}, f32[256,3,128]{2,0,1:T(8,128)S(1)}, u32[]{:S(2)}, u32[]{:S(2)}) %collective-permute-start.3) | collective-permute-done | bytes 393248 | tf_op jit(solution)/shard_map/ppermute | solution.py:16
  673.0 17.9 %all_to_all.67 = f32[8,32,384]{2,1,0:T(8,128)S(1)} all-to-all(f32[8,32,384]{2,1,0:T(8,128)S(1)} %all_to_all.59), channel_id=1, replica_groups=mesh['head'=8,'blk'=32] {'head'}, dimensions={0} | all-to-all | bytes 786432 | tf_op jit(solution)/shard_map/all_to_all | solution.py:117
  (484 shorter events, 117.0 us)
Async XLA Ops:
  88.2 20.1 %collective-permute-start.1 = (f32[256,3,128]{2,0,1:T(8,128)S(1)}, f32[256,3,128]{2,0,1:T(8,128)S(1)}, u32[]{:S(2)}, u32[]{:S(2)}) collective-permute-start(f32[256,3,128]{2,0,1:T(8,128)S(1)} %get-tuple-element.396), channel_id=1, source_target_pairs={{31,0},{0,1},{1,2},{2,3},{3,4},{4,5},{5,6},{6,7},{7,8},{8,9},{9,10... | collective-permute-start | bytes 1179656 | tf_op jit(solution)/shard_map/while/body/eval_jaxpr/ppermute | solution.py:16
  112.1 18.9 %collective-permute-start.1 = (f32[256,3,128]{2,0,1:T(8,128)S(1)}, f32[256,3,128]{2,0,1:T(8,128)S(1)}, u32[]{:S(2)}, u32[]{:S(2)}) collective-permute-start(f32[256,3,128]{2,0,1:T(8,128)S(1)} %get-tuple-element.396), channel_id=1, source_target_pairs={{31,0},{0,1},{1,2},{2,3},{3,4},{4,5},{5,6},{6,7},{7,8},{8,9},{9,10... | collective-permute-start | bytes 1179656 | tf_op jit(solution)/shard_map/while/body/eval_jaxpr/ppermute | solution.py:16
  173.7 17.8 %collective-permute-start.1 = (f32[256,3,128]{2,0,1:T(8,128)S(1)}, f32[256,3,128]{2,0,1:T(8,128)S(1)}, u32[]{:S(2)}, u32[]{:S(2)}) collective-permute-start(f32[256,3,128]{2,0,1:T(8,128)S(1)} %get-tuple-element.396), channel_id=1, source_target_pairs={{31,0},{0,1},{1,2},{2,3},{3,4},{4,5},{5,6},{6,7},{7,8},{8,9},{9,10... | collective-permute-start | bytes 1179656 | tf_op jit(solution)/shard_map/while/body/eval_jaxpr/ppermute | solution.py:16
  173.8 17.8 %collective-permute-start = (bf16[256,3,128]{2,0,1:T(8,128)(2,1)S(1)}, bf16[256,3,128]{2,0,1:T(8,128)(2,1)S(1)}, u32[]{:S(2)}, u32[]{:S(2)}) collective-permute-start(bf16[256,3,128]{2,0,1:T(8,128)(2,1)S(1)} %copy.69), channel_id=1, source_target_pairs={{31,0},{0,1},{1,2},{2,3},{3,4},{4,5},{5,6},{6,7},{7,8},{8,9},{9,10... | collective-permute-start | bytes 589832 | tf_op jit(solution)/shard_map/while/body/eval_jaxpr/ppermute | solution.py:16
  173.9 17.6 %collective-permute-start.2 = (f32[3,256]{1,0:T(4,128)S(1)}, f32[3,256]{1,0:T(4,128)S(1)}, u32[]{:S(2)}, u32[]{:S(2)}) collective-permute-start(f32[3,256]{1,0:T(4,128)S(1)} %get-tuple-element.397), channel_id=1, source_target_pairs={{31,0},{0,1},{1,2},{2,3},{3,4},{4,5},{5,6},{6,7},{7,8},{8,9},{9,10... | collective-permute-start | bytes 9224 | tf_op jit(solution)/shard_map/while/body/eval_jaxpr/ppermute | solution.py:16
  212.8 18.7 %collective-permute-start.1 = (f32[256,3,128]{2,0,1:T(8,128)S(1)}, f32[256,3,128]{2,0,1:T(8,128)S(1)}, u32[]{:S(2)}, u32[]{:S(2)}) collective-permute-start(f32[256,3,128]{2,0,1:T(8,128)S(1)} %get-tuple-element.396), channel_id=1, source_target_pairs={{31,0},{0,1},{1,2},{2,3},{3,4},{4,5},{5,6},{6,7},{7,8},{8,9},{9,10... | collective-permute-start | bytes 1179656 | tf_op jit(solution)/shard_map/while/body/eval_jaxpr/ppermute | solution.py:16
  212.9 18.7 %collective-permute-start = (bf16[256,3,128]{2,0,1:T(8,128)(2,1)S(1)}, bf16[256,3,128]{2,0,1:T(8,128)(2,1)S(1)}, u32[]{:S(2)}, u32[]{:S(2)}) collective-permute-start(bf16[256,3,128]{2,0,1:T(8,128)(2,1)S(1)} %copy.69), channel_id=1, source_target_pairs={{31,0},{0,1},{1,2},{2,3},{3,4},{4,5},{5,6},{6,7},{7,8},{8,9},{9,10... | collective-permute-start | bytes 589832 | tf_op jit(solution)/shard_map/while/body/eval_jaxpr/ppermute | solution.py:16
  212.9 18.5 %collective-permute-start.2 = (f32[3,256]{1,0:T(4,128)S(1)}, f32[3,256]{1,0:T(4,128)S(1)}, u32[]{:S(2)}, u32[]{:S(2)}) collective-permute-start(f32[3,256]{1,0:T(4,128)S(1)} %get-tuple-element.397), channel_id=1, source_target_pairs={{31,0},{0,1},{1,2},{2,3},{3,4},{4,5},{5,6},{6,7},{7,8},{8,9},{9,10... | collective-permute-start | bytes 9224 | tf_op jit(solution)/shard_map/while/body/eval_jaxpr/ppermute | solution.py:16
  233.7 18.8 %collective-permute-start.1 = (f32[256,3,128]{2,0,1:T(8,128)S(1)}, f32[256,3,128]{2,0,1:T(8,128)S(1)}, u32[]{:S(2)}, u32[]{:S(2)}) collective-permute-start(f32[256,3,128]{2,0,1:T(8,128)S(1)} %get-tuple-element.396), channel_id=1, source_target_pairs={{31,0},{0,1},{1,2},{2,3},{3,4},{4,5},{5,6},{6,7},{7,8},{8,9},{9,10... | collective-permute-start | bytes 1179656 | tf_op jit(solution)/shard_map/while/body/eval_jaxpr/ppermute | solution.py:16
  233.8 18.7 %collective-permute-start = (bf16[256,3,128]{2,0,1:T(8,128)(2,1)S(1)}, bf16[256,3,128]{2,0,1:T(8,128)(2,1)S(1)}, u32[]{:S(2)}, u32[]{:S(2)}) collective-permute-start(bf16[256,3,128]{2,0,1:T(8,128)(2,1)S(1)} %copy.69), channel_id=1, source_target_pairs={{31,0},{0,1},{1,2},{2,3},{3,4},{4,5},{5,6},{6,7},{7,8},{8,9},{9,10... | collective-permute-start | bytes 589832 | tf_op jit(solution)/shard_map/while/body/eval_jaxpr/ppermute | solution.py:16
  233.8 18.6 %collective-permute-start.2 = (f32[3,256]{1,0:T(4,128)S(1)}, f32[3,256]{1,0:T(4,128)S(1)}, u32[]{:S(2)}, u32[]{:S(2)}) collective-permute-start(f32[3,256]{1,0:T(4,128)S(1)} %get-tuple-element.397), channel_id=1, source_target_pairs={{31,0},{0,1},{1,2},{2,3},{3,4},{4,5},{5,6},{6,7},{7,8},{8,9},{9,10... | collective-permute-start | bytes 9224 | tf_op jit(solution)/shard_map/while/body/eval_jaxpr/ppermute | solution.py:16
  254.6 18.0 %collective-permute-start.1 = (f32[256,3,128]{2,0,1:T(8,128)S(1)}, f32[256,3,128]{2,0,1:T(8,128)S(1)}, u32[]{:S(2)}, u32[]{:S(2)}) collective-permute-start(f32[256,3,128]{2,0,1:T(8,128)S(1)} %get-tuple-element.396), channel_id=1, source_target_pairs={{31,0},{0,1},{1,2},{2,3},{3,4},{4,5},{5,6},{6,7},{7,8},{8,9},{9,10... | collective-permute-start | bytes 1179656 | tf_op jit(solution)/shard_map/while/body/eval_jaxpr/ppermute | solution.py:16
  254.7 17.9 %collective-permute-start = (bf16[256,3,128]{2,0,1:T(8,128)(2,1)S(1)}, bf16[256,3,128]{2,0,1:T(8,128)(2,1)S(1)}, u32[]{:S(2)}, u32[]{:S(2)}) collective-permute-start(bf16[256,3,128]{2,0,1:T(8,128)(2,1)S(1)} %copy.69), channel_id=1, source_target_pairs={{31,0},{0,1},{1,2},{2,3},{3,4},{4,5},{5,6},{6,7},{7,8},{8,9},{9,10... | collective-permute-start | bytes 589832 | tf_op jit(solution)/shard_map/while/body/eval_jaxpr/ppermute | solution.py:16
  254.8 17.8 %collective-permute-start.2 = (f32[3,256]{1,0:T(4,128)S(1)}, f32[3,256]{1,0:T(4,128)S(1)}, u32[]{:S(2)}, u32[]{:S(2)}) collective-permute-start(f32[3,256]{1,0:T(4,128)S(1)} %get-tuple-element.397), channel_id=1, source_target_pairs={{31,0},{0,1},{1,2},{2,3},{3,4},{4,5},{5,6},{6,7},{7,8},{8,9},{9,10... | collective-permute-start | bytes 9224 | tf_op jit(solution)/shard_map/while/body/eval_jaxpr/ppermute | solution.py:16
  274.8 18.7 %collective-permute-start.1 = (f32[256,3,128]{2,0,1:T(8,128)S(1)}, f32[256,3,128]{2,0,1:T(8,128)S(1)}, u32[]{:S(2)}, u32[]{:S(2)}) collective-permute-start(f32[256,3,128]{2,0,1:T(8,128)S(1)} %get-tuple-element.396), channel_id=1, source_target_pairs={{31,0},{0,1},{1,2},{2,3},{3,4},{4,5},{5,6},{6,7},{7,8},{8,9},{9,10... | collective-permute-start | bytes 1179656 | tf_op jit(solution)/shard_map/while/body/eval_jaxpr/ppermute | solution.py:16
  274.9 18.7 %collective-permute-start = (bf16[256,3,128]{2,0,1:T(8,128)(2,1)S(1)}, bf16[256,3,128]{2,0,1:T(8,128)(2,1)S(1)}, u32[]{:S(2)}, u32[]{:S(2)}) collective-permute-start(bf16[256,3,128]{2,0,1:T(8,128)(2,1)S(1)} %copy.69), channel_id=1, source_target_pairs={{31,0},{0,1},{1,2},{2,3},{3,4},{4,5},{5,6},{6,7},{7,8},{8,9},{9,10... | collective-permute-start | bytes 589832 | tf_op jit(solution)/shard_map/while/body/eval_jaxpr/ppermute | solution.py:16
  275.0 18.5 %collective-permute-start.2 = (f32[3,256]{1,0:T(4,128)S(1)}, f32[3,256]{1,0:T(4,128)S(1)}, u32[]{:S(2)}, u32[]{:S(2)}) collective-permute-start(f32[3,256]{1,0:T(4,128)S(1)} %get-tuple-element.397), channel_id=1, source_target_pairs={{31,0},{0,1},{1,2},{2,3},{3,4},{4,5},{5,6},{6,7},{7,8},{8,9},{9,10... | collective-permute-start | bytes 9224 | tf_op jit(solution)/shard_map/while/body/eval_jaxpr/ppermute | solution.py:16
  314.6 18.8 %collective-permute-start.1 = (f32[256,3,128]{2,0,1:T(8,128)S(1)}, f32[256,3,128]{2,0,1:T(8,128)S(1)}, u32[]{:S(2)}, u32[]{:S(2)}) collective-permute-start(f32[256,3,128]{2,0,1:T(8,128)S(1)} %get-tuple-element.396), channel_id=1, source_target_pairs={{31,0},{0,1},{1,2},{2,3},{3,4},{4,5},{5,6},{6,7},{7,8},{8,9},{9,10... | collective-permute-start | bytes 1179656 | tf_op jit(solution)/shard_map/while/body/eval_jaxpr/ppermute | solution.py:16
  314.7 18.7 %collective-permute-start = (bf16[256,3,128]{2,0,1:T(8,128)(2,1)S(1)}, bf16[256,3,128]{2,0,1:T(8,128)(2,1)S(1)}, u32[]{:S(2)}, u32[]{:S(2)}) collective-permute-start(bf16[256,3,128]{2,0,1:T(8,128)(2,1)S(1)} %copy.69), channel_id=1, source_target_pairs={{31,0},{0,1},{1,2},{2,3},{3,4},{4,5},{5,6},{6,7},{7,8},{8,9},{9,10... | collective-permute-start | bytes 589832 | tf_op jit(solution)/shard_map/while/body/eval_jaxpr/ppermute | solution.py:16
  314.8 18.6 %collective-permute-start.2 = (f32[3,256]{1,0:T(4,128)S(1)}, f32[3,256]{1,0:T(4,128)S(1)}, u32[]{:S(2)}, u32[]{:S(2)}) collective-permute-start(f32[3,256]{1,0:T(4,128)S(1)} %get-tuple-element.397), channel_id=1, source_target_pairs={{31,0},{0,1},{1,2},{2,3},{3,4},{4,5},{5,6},{6,7},{7,8},{8,9},{9,10... | collective-permute-start | bytes 9224 | tf_op jit(solution)/shard_map/while/body/eval_jaxpr/ppermute | solution.py:16
  335.6 18.0 %collective-permute-start.1 = (f32[256,3,128]{2,0,1:T(8,128)S(1)}, f32[256,3,128]{2,0,1:T(8,128)S(1)}, u32[]{:S(2)}, u32[]{:S(2)}) collective-permute-start(f32[256,3,128]{2,0,1:T(8,128)S(1)} %get-tuple-element.396), channel_id=1, source_target_pairs={{31,0},{0,1},{1,2},{2,3},{3,4},{4,5},{5,6},{6,7},{7,8},{8,9},{9,10... | collective-permute-start | bytes 1179656 | tf_op jit(solution)/shard_map/while/body/eval_jaxpr/ppermute | solution.py:16
  335.7 17.9 %collective-permute-start = (bf16[256,3,128]{2,0,1:T(8,128)(2,1)S(1)}, bf16[256,3,128]{2,0,1:T(8,128)(2,1)S(1)}, u32[]{:S(2)}, u32[]{:S(2)}) collective-permute-start(bf16[256,3,128]{2,0,1:T(8,128)(2,1)S(1)} %copy.69), channel_id=1, source_target_pairs={{31,0},{0,1},{1,2},{2,3},{3,4},{4,5},{5,6},{6,7},{7,8},{8,9},{9,10... | collective-permute-start | bytes 589832 | tf_op jit(solution)/shard_map/while/body/eval_jaxpr/ppermute | solution.py:16
  335.8 17.8 %collective-permute-start.2 = (f32[3,256]{1,0:T(4,128)S(1)}, f32[3,256]{1,0:T(4,128)S(1)}, u32[]{:S(2)}, u32[]{:S(2)}) collective-permute-start(f32[3,256]{1,0:T(4,128)S(1)} %get-tuple-element.397), channel_id=1, source_target_pairs={{31,0},{0,1},{1,2},{2,3},{3,4},{4,5},{5,6},{6,7},{7,8},{8,9},{9,10... | collective-permute-start | bytes 9224 | tf_op jit(solution)/shard_map/while/body/eval_jaxpr/ppermute | solution.py:16
  355.7 17.6 %collective-permute-start.1 = (f32[256,3,128]{2,0,1:T(8,128)S(1)}, f32[256,3,128]{2,0,1:T(8,128)S(1)}, u32[]{:S(2)}, u32[]{:S(2)}) collective-permute-start(f32[256,3,128]{2,0,1:T(8,128)S(1)} %get-tuple-element.396), channel_id=1, source_target_pairs={{31,0},{0,1},{1,2},{2,3},{3,4},{4,5},{5,6},{6,7},{7,8},{8,9},{9,10... | collective-permute-start | bytes 1179656 | tf_op jit(solution)/shard_map/while/body/eval_jaxpr/ppermute | solution.py:16
  355.8 17.6 %collective-permute-start = (bf16[256,3,128]{2,0,1:T(8,128)(2,1)S(1)}, bf16[256,3,128]{2,0,1:T(8,128)(2,1)S(1)}, u32[]{:S(2)}, u32[]{:S(2)}) collective-permute-start(bf16[256,3,128]{2,0,1:T(8,128)(2,1)S(1)} %copy.69), channel_id=1, source_target_pairs={{31,0},{0,1},{1,2},{2,3},{3,4},{4,5},{5,6},{6,7},{7,8},{8,9},{9,10... | collective-permute-start | bytes 589832 | tf_op jit(solution)/shard_map/while/body/eval_jaxpr/ppermute | solution.py:16
  355.9 17.4 %collective-permute-start.2 = (f32[3,256]{1,0:T(4,128)S(1)}, f32[3,256]{1,0:T(4,128)S(1)}, u32[]{:S(2)}, u32[]{:S(2)}) collective-permute-start(f32[3,256]{1,0:T(4,128)S(1)} %get-tuple-element.397), channel_id=1, source_target_pairs={{31,0},{0,1},{1,2},{2,3},{3,4},{4,5},{5,6},{6,7},{7,8},{8,9},{9,10... | collective-permute-start | bytes 9224 | tf_op jit(solution)/shard_map/while/body/eval_jaxpr/ppermute | solution.py:16
  375.5 18.6 %collective-permute-start.1 = (f32[256,3,128]{2,0,1:T(8,128)S(1)}, f32[256,3,128]{2,0,1:T(8,128)S(1)}, u32[]{:S(2)}, u32[]{:S(2)}) collective-permute-start(f32[256,3,128]{2,0,1:T(8,128)S(1)} %get-tuple-element.396), channel_id=1, source_target_pairs={{31,0},{0,1},{1,2},{2,3},{3,4},{4,5},{5,6},{6,7},{7,8},{8,9},{9,10... | collective-permute-start | bytes 1179656 | tf_op jit(solution)/shard_map/while/body/eval_jaxpr/ppermute | solution.py:16
  375.6 18.6 %collective-permute-start = (bf16[256,3,128]{2,0,1:T(8,128)(2,1)S(1)}, bf16[256,3,128]{2,0,1:T(8,128)(2,1)S(1)}, u32[]{:S(2)}, u32[]{:S(2)}) collective-permute-start(bf16[256,3,128]{2,0,1:T(8,128)(2,1)S(1)} %copy.69), channel_id=1, source_target_pairs={{31,0},{0,1},{1,2},{2,3},{3,4},{4,5},{5,6},{6,7},{7,8},{8,9},{9,10... | collective-permute-start | bytes 589832 | tf_op jit(solution)/shard_map/while/body/eval_jaxpr/ppermute | solution.py:16
  375.7 18.4 %collective-permute-start.2 = (f32[3,256]{1,0:T(4,128)S(1)}, f32[3,256]{1,0:T(4,128)S(1)}, u32[]{:S(2)}, u32[]{:S(2)}) collective-permute-start(f32[3,256]{1,0:T(4,128)S(1)} %get-tuple-element.397), channel_id=1, source_target_pairs={{31,0},{0,1},{1,2},{2,3},{3,4},{4,5},{5,6},{6,7},{7,8},{8,9},{9,10... | collective-permute-start | bytes 9224 | tf_op jit(solution)/shard_map/while/body/eval_jaxpr/ppermute | solution.py:16
  396.3 18.2 %collective-permute-start.1 = (f32[256,3,128]{2,0,1:T(8,128)S(1)}, f32[256,3,128]{2,0,1:T(8,128)S(1)}, u32[]{:S(2)}, u32[]{:S(2)}) collective-permute-start(f32[256,3,128]{2,0,1:T(8,128)S(1)} %get-tuple-element.396), channel_id=1, source_target_pairs={{31,0},{0,1},{1,2},{2,3},{3,4},{4,5},{5,6},{6,7},{7,8},{8,9},{9,10... | collective-permute-start | bytes 1179656 | tf_op jit(solution)/shard_map/while/body/eval_jaxpr/ppermute | solution.py:16
  396.4 18.2 %collective-permute-start = (bf16[256,3,128]{2,0,1:T(8,128)(2,1)S(1)}, bf16[256,3,128]{2,0,1:T(8,128)(2,1)S(1)}, u32[]{:S(2)}, u32[]{:S(2)}) collective-permute-start(bf16[256,3,128]{2,0,1:T(8,128)(2,1)S(1)} %copy.69), channel_id=1, source_target_pairs={{31,0},{0,1},{1,2},{2,3},{3,4},{4,5},{5,6},{6,7},{7,8},{8,9},{9,10... | collective-permute-start | bytes 589832 | tf_op jit(solution)/shard_map/while/body/eval_jaxpr/ppermute | solution.py:16
  396.5 18.0 %collective-permute-start.2 = (f32[3,256]{1,0:T(4,128)S(1)}, f32[3,256]{1,0:T(4,128)S(1)}, u32[]{:S(2)}, u32[]{:S(2)}) collective-permute-start(f32[3,256]{1,0:T(4,128)S(1)} %get-tuple-element.397), channel_id=1, source_target_pairs={{31,0},{0,1},{1,2},{2,3},{3,4},{4,5},{5,6},{6,7},{7,8},{8,9},{9,10... | collective-permute-start | bytes 9224 | tf_op jit(solution)/shard_map/while/body/eval_jaxpr/ppermute | solution.py:16
  457.6 17.8 %collective-permute-start.1 = (f32[256,3,128]{2,0,1:T(8,128)S(1)}, f32[256,3,128]{2,0,1:T(8,128)S(1)}, u32[]{:S(2)}, u32[]{:S(2)}) collective-permute-start(f32[256,3,128]{2,0,1:T(8,128)S(1)} %get-tuple-element.396), channel_id=1, source_target_pairs={{31,0},{0,1},{1,2},{2,3},{3,4},{4,5},{5,6},{6,7},{7,8},{8,9},{9,10... | collective-permute-start | bytes 1179656 | tf_op jit(solution)/shard_map/while/body/eval_jaxpr/ppermute | solution.py:16
  457.7 17.7 %collective-permute-start = (bf16[256,3,128]{2,0,1:T(8,128)(2,1)S(1)}, bf16[256,3,128]{2,0,1:T(8,128)(2,1)S(1)}, u32[]{:S(2)}, u32[]{:S(2)}) collective-permute-start(bf16[256,3,128]{2,0,1:T(8,128)(2,1)S(1)} %copy.69), channel_id=1, source_target_pairs={{31,0},{0,1},{1,2},{2,3},{3,4},{4,5},{5,6},{6,7},{7,8},{8,9},{9,10... | collective-permute-start | bytes 589832 | tf_op jit(solution)/shard_map/while/body/eval_jaxpr/ppermute | solution.py:16
  457.8 17.6 %collective-permute-start.2 = (f32[3,256]{1,0:T(4,128)S(1)}, f32[3,256]{1,0:T(4,128)S(1)}, u32[]{:S(2)}, u32[]{:S(2)}) collective-permute-start(f32[3,256]{1,0:T(4,128)S(1)} %get-tuple-element.397), channel_id=1, source_target_pairs={{31,0},{0,1},{1,2},{2,3},{3,4},{4,5},{5,6},{6,7},{7,8},{8,9},{9,10... | collective-permute-start | bytes 9224 | tf_op jit(solution)/shard_map/while/body/eval_jaxpr/ppermute | solution.py:16
  479.2 17.7 %collective-permute-start.1 = (f32[256,3,128]{2,0,1:T(8,128)S(1)}, f32[256,3,128]{2,0,1:T(8,128)S(1)}, u32[]{:S(2)}, u32[]{:S(2)}) collective-permute-start(f32[256,3,128]{2,0,1:T(8,128)S(1)} %get-tuple-element.396), channel_id=1, source_target_pairs={{31,0},{0,1},{1,2},{2,3},{3,4},{4,5},{5,6},{6,7},{7,8},{8,9},{9,10... | collective-permute-start | bytes 1179656 | tf_op jit(solution)/shard_map/while/body/eval_jaxpr/ppermute | solution.py:16
  479.3 17.6 %collective-permute-start = (bf16[256,3,128]{2,0,1:T(8,128)(2,1)S(1)}, bf16[256,3,128]{2,0,1:T(8,128)(2,1)S(1)}, u32[]{:S(2)}, u32[]{:S(2)}) collective-permute-start(bf16[256,3,128]{2,0,1:T(8,128)(2,1)S(1)} %copy.69), channel_id=1, source_target_pairs={{31,0},{0,1},{1,2},{2,3},{3,4},{4,5},{5,6},{6,7},{7,8},{8,9},{9,10... | collective-permute-start | bytes 589832 | tf_op jit(solution)/shard_map/while/body/eval_jaxpr/ppermute | solution.py:16
  479.3 17.5 %collective-permute-start.2 = (f32[3,256]{1,0:T(4,128)S(1)}, f32[3,256]{1,0:T(4,128)S(1)}, u32[]{:S(2)}, u32[]{:S(2)}) collective-permute-start(f32[3,256]{1,0:T(4,128)S(1)} %get-tuple-element.397), channel_id=1, source_target_pairs={{31,0},{0,1},{1,2},{2,3},{3,4},{4,5},{5,6},{6,7},{7,8},{8,9},{9,10... | collective-permute-start | bytes 9224 | tf_op jit(solution)/shard_map/while/body/eval_jaxpr/ppermute | solution.py:16
  537.6 18.1 %collective-permute-start.1 = (f32[256,3,128]{2,0,1:T(8,128)S(1)}, f32[256,3,128]{2,0,1:T(8,128)S(1)}, u32[]{:S(2)}, u32[]{:S(2)}) collective-permute-start(f32[256,3,128]{2,0,1:T(8,128)S(1)} %get-tuple-element.396), channel_id=1, source_target_pairs={{31,0},{0,1},{1,2},{2,3},{3,4},{4,5},{5,6},{6,7},{7,8},{8,9},{9,10... | collective-permute-start | bytes 1179656 | tf_op jit(solution)/shard_map/while/body/eval_jaxpr/ppermute | solution.py:16
  537.7 18.1 %collective-permute-start = (bf16[256,3,128]{2,0,1:T(8,128)(2,1)S(1)}, bf16[256,3,128]{2,0,1:T(8,128)(2,1)S(1)}, u32[]{:S(2)}, u32[]{:S(2)}) collective-permute-start(bf16[256,3,128]{2,0,1:T(8,128)(2,1)S(1)} %copy.69), channel_id=1, source_target_pairs={{31,0},{0,1},{1,2},{2,3},{3,4},{4,5},{5,6},{6,7},{7,8},{8,9},{9,10... | collective-permute-start | bytes 589832 | tf_op jit(solution)/shard_map/while/body/eval_jaxpr/ppermute | solution.py:16
  537.8 17.9 %collective-permute-start.2 = (f32[3,256]{1,0:T(4,128)S(1)}, f32[3,256]{1,0:T(4,128)S(1)}, u32[]{:S(2)}, u32[]{:S(2)}) collective-permute-start(f32[3,256]{1,0:T(4,128)S(1)} %get-tuple-element.397), channel_id=1, source_target_pairs={{31,0},{0,1},{1,2},{2,3},{3,4},{4,5},{5,6},{6,7},{7,8},{8,9},{9,10... | collective-permute-start | bytes 9224 | tf_op jit(solution)/shard_map/while/body/eval_jaxpr/ppermute | solution.py:16
  557.9 18.7 %collective-permute-start.1 = (f32[256,3,128]{2,0,1:T(8,128)S(1)}, f32[256,3,128]{2,0,1:T(8,128)S(1)}, u32[]{:S(2)}, u32[]{:S(2)}) collective-permute-start(f32[256,3,128]{2,0,1:T(8,128)S(1)} %get-tuple-element.396), channel_id=1, source_target_pairs={{31,0},{0,1},{1,2},{2,3},{3,4},{4,5},{5,6},{6,7},{7,8},{8,9},{9,10... | collective-permute-start | bytes 1179656 | tf_op jit(solution)/shard_map/while/body/eval_jaxpr/ppermute | solution.py:16
  558.0 18.6 %collective-permute-start = (bf16[256,3,128]{2,0,1:T(8,128)(2,1)S(1)}, bf16[256,3,128]{2,0,1:T(8,128)(2,1)S(1)}, u32[]{:S(2)}, u32[]{:S(2)}) collective-permute-start(bf16[256,3,128]{2,0,1:T(8,128)(2,1)S(1)} %copy.69), channel_id=1, source_target_pairs={{31,0},{0,1},{1,2},{2,3},{3,4},{4,5},{5,6},{6,7},{7,8},{8,9},{9,10... | collective-permute-start | bytes 589832 | tf_op jit(solution)/shard_map/while/body/eval_jaxpr/ppermute | solution.py:16
  558.1 18.5 %collective-permute-start.2 = (f32[3,256]{1,0:T(4,128)S(1)}, f32[3,256]{1,0:T(4,128)S(1)}, u32[]{:S(2)}, u32[]{:S(2)}) collective-permute-start(f32[3,256]{1,0:T(4,128)S(1)} %get-tuple-element.397), channel_id=1, source_target_pairs={{31,0},{0,1},{1,2},{2,3},{3,4},{4,5},{5,6},{6,7},{7,8},{8,9},{9,10... | collective-permute-start | bytes 9224 | tf_op jit(solution)/shard_map/while/body/eval_jaxpr/ppermute | solution.py:16
  619.3 17.1 %collective-permute-start.1 = (f32[256,3,128]{2,0,1:T(8,128)S(1)}, f32[256,3,128]{2,0,1:T(8,128)S(1)}, u32[]{:S(2)}, u32[]{:S(2)}) collective-permute-start(f32[256,3,128]{2,0,1:T(8,128)S(1)} %get-tuple-element.396), channel_id=1, source_target_pairs={{31,0},{0,1},{1,2},{2,3},{3,4},{4,5},{5,6},{6,7},{7,8},{8,9},{9,10... | collective-permute-start | bytes 1179656 | tf_op jit(solution)/shard_map/while/body/eval_jaxpr/ppermute | solution.py:16
  640.1 18.4 %collective-permute-start.1 = (f32[256,3,128]{2,0,1:T(8,128)S(1)}, f32[256,3,128]{2,0,1:T(8,128)S(1)}, u32[]{:S(2)}, u32[]{:S(2)}) collective-permute-start(f32[256,3,128]{2,0,1:T(8,128)S(1)} %get-tuple-element.396), channel_id=1, source_target_pairs={{31,0},{0,1},{1,2},{2,3},{3,4},{4,5},{5,6},{6,7},{7,8},{8,9},{9,10... | collective-permute-start | bytes 1179656 | tf_op jit(solution)/shard_map/while/body/eval_jaxpr/ppermute | solution.py:16
  640.2 18.3 %collective-permute-start = (bf16[256,3,128]{2,0,1:T(8,128)(2,1)S(1)}, bf16[256,3,128]{2,0,1:T(8,128)(2,1)S(1)}, u32[]{:S(2)}, u32[]{:S(2)}) collective-permute-start(bf16[256,3,128]{2,0,1:T(8,128)(2,1)S(1)} %copy.69), channel_id=1, source_target_pairs={{31,0},{0,1},{1,2},{2,3},{3,4},{4,5},{5,6},{6,7},{7,8},{8,9},{9,10... | collective-permute-start | bytes 589832 | tf_op jit(solution)/shard_map/while/body/eval_jaxpr/ppermute | solution.py:16
  640.3 18.2 %collective-permute-start.2 = (f32[3,256]{1,0:T(4,128)S(1)}, f32[3,256]{1,0:T(4,128)S(1)}, u32[]{:S(2)}, u32[]{:S(2)}) collective-permute-start(f32[3,256]{1,0:T(4,128)S(1)} %get-tuple-element.397), channel_id=1, source_target_pairs={{31,0},{0,1},{1,2},{2,3},{3,4},{4,5},{5,6},{6,7},{7,8},{8,9},{9,10... | collective-permute-start | bytes 9224 | tf_op jit(solution)/shard_map/while/body/eval_jaxpr/ppermute | solution.py:16
  (51 other events, 722.6 us)
where the time goes:
time: 693 us; the launch traced here: 692 us
  waiting for transfers between devices  510 us (74%)
  starting transfers between devices  60.3 us (9%)
  other arithmetic  48.9 us (7%)
  loops' own time  24.2 us (3%)
  blocking collectives  17.9 us (3%)
  matrix products  17.8 us (3%)
  local copies, waits for them, and re-layouts  12.1 us (2%)
    ppermute x94, waiting for transfers between devices, passed_along(): return lax.ppermute(block, axis, route)  493 us
    ppermute x94, starting transfers between devices, passed_along(): return lax.ppermute(block, axis, route)  47.6 us
    reduce_or x32, other arithmetic, visit_block(): return lax.cond(jnp.any(tile_block > 0), include, unchanged, carried_state)  45 us
    another operation x1, loops' own time, local(): lax.fori_loop(0, cycle_size - 1, cycle_turn, (query_block, initial[0], in...  23.1 us
    all_to_all x1, blocking collectives, local(): lax.all_to_all(attended, 'head', split_axis=0, concat_axis=1, tiled=True)  17.9 us
  transfers between devices with their start and end apart: 97, of which 35 were waited for; matrix products, arithmetic and copies ran while one was open for 1% of the time, Pallas kernels for 0%

commit v1 on v0

v1 whole, which is shorter than its diff:
```python
import functools

import jax
import jax.numpy as jnp
from jax import lax
from jax.experimental import pallas as pl
from jax.experimental.pallas import tpu as pltpu
from jax.sharding import PartitionSpec as P

MESH = pl.DeviceIdType.MESH

HEADS = 24
HEAD_DIM = 128
TILE = 128
PIECE = 32
LEVELS = 4
HALF = 1024
QUARTER = HALF // 2
BLOCK = 256
MASKED = -1e30
SCALE2 = HEAD_DIM**-0.5 * 1.4426950408889634


def place():
    head, blk = lax.axis_index("head"), lax.axis_index("blk")
    return head // 2, blk // 8, (blk // 2) % 4, head % 2, blk % 2


def column_of(head):
    return head // 8, head % 8


def device_at(x, y, z, core):
    return (x * 2 + z % 2, y * 8 + (z // 2) * 2 + core)


def kernel(
    q_ref, k_ref, v_ref, mask_ref, out_ref,
    mask, qa, kv, hot, peak, acc, obuf,
    in_sem, in_send, self_sem, y_recv, y_send, sib_recv, sib_send, o_recv, o_send, mask_sem,
):
    x, y, zh, zl, core = place()
    z = zh * 2 + zl
    me = x * 8 + z
    busy = x < 3
    slot = (zh * 8 + x * 2 + zl) * PIECE
    up, down = (y + 1) % 4, (y + 3) % 4
    sources = (k_ref, v_ref, q_ref)

    barrier = pltpu.get_barrier_semaphore()

    def greet(i, _):
        other = (me + i) % 32
        pl.semaphore_signal(
            barrier, inc=1, device_id=device_at(other // 8, y, other % 8, core), device_id_type=MESH
        )
        return 0

    lax.fori_loop(1, 32, greet, 0)
    for there in (
        device_at(x, up, z, core), device_at(x, down, z, core), device_at(x, y, z, 1 - core),
    ):
        pl.semaphore_signal(barrier, inc=1, device_id=there, device_id_type=MESH)
    pl.semaphore_wait(barrier, 34)

    mask_copy = pltpu.make_async_copy(mask_ref, mask, mask_sem)
    mask_copy.start()

    def landing(n):
        if n == 2:
            return qa.at[pl.ds(slot, PIECE), pl.ds(0, HEAD_DIM)]
        return kv.at[n, y, core, pl.ds(slot, PIECE), :]

    for n in range(3):

        def send_piece(i, _, n=n):
            head = (me + i) % HEADS
            hx, hz = column_of(head)
            source = sources[n].at[:, pl.ds(pl.multiple_of(head * HEAD_DIM, HEAD_DIM), HEAD_DIM)]

            @pl.when(head != me)
            def _():
                pltpu.make_async_remote_copy(
                    src_ref=source, dst_ref=landing(n), send_sem=in_send.at[n], recv_sem=in_sem.at[n],
                    device_id=device_at(hx, y, hz, core), device_id_type=MESH,
                ).start()

            @pl.when(head == me)
            def _():
                pltpu.make_async_copy(source, landing(n), self_sem.at[n]).start()

            return 0

        lax.fori_loop(0, HEADS, send_piece, 0)

    def wait_pieces(n):
        whole = kv.at[0, 0, 0, pl.ds(0, HALF - PIECE), :]
        pltpu.make_async_copy(whole, whole, in_sem.at[n]).wait()
        pltpu.make_async_copy(landing(n), landing(n), self_sem.at[n]).wait()

    def y_copy(n, level, half, step, up_way):
        part = kv.at[n, level, core, pl.ds(half * QUARTER, QUARTER), :]
        return pltpu.make_async_remote_copy(
            src_ref=part, dst_ref=part, send_sem=y_send.at[n, step, half, int(up_way)],
            recv_sem=y_recv.at[n, step, half, int(up_way)],
            device_id=device_at(x, up if up_way else down, z, core), device_id_type=MESH,
        )

    def sib_copy(n, step, half, from_me=True):
        level = ((y, down, up, (y + 2) % 4))[step]
        whose = core if from_me else 1 - core
        part = kv.at[n, level, whose, pl.ds(half * QUARTER, QUARTER), :]
        return pltpu.make_async_remote_copy(
            src_ref=part, dst_ref=part, send_sem=sib_send.at[n, step, half],
            recv_sem=sib_recv.at[n, step, half],
            device_id=device_at(x, y, z, 1 - core), device_id_type=MESH,
        )

    def visit(step, whose, q_block):
        level = ((y, down, up, (y + 2) % 4))[step]
        rows = pl.ds(pl.multiple_of(q_block * BLOCK, BLOCK), BLOCK)
        keys = jnp.concatenate([kv[0, level, whose], hot[level, whose]], axis=1)
        scores = lax.dot_general(
            qa[rows, :], keys, (((1,), (1,)), ((), ())), preferred_element_type=jnp.float32
        )
        before = peak[rows, :]
        now = jnp.maximum(before, jnp.max(scores, axis=1, keepdims=True))
        peak[rows, :] = now
        weights = jnp.exp2((scores - now[:, :1]) * SCALE2).astype(jnp.bfloat16)
        fade = jnp.exp2((before - now) * SCALE2)
        vals = jnp.concatenate(
            [kv[1, level, whose], jnp.ones((HALF, HEAD_DIM), jnp.bfloat16)], axis=1
        )
        mixed = jnp.dot(weights, vals, preferred_element_type=jnp.float32)
        acc[rows, :] = acc[rows, :] * jnp.concatenate([fade, fade], axis=1) + mixed

    def visit_all(step, whose):
        def one(q_block, _):
            visit(step, whose, q_block)
            return 0

        lax.fori_loop(0, HALF // BLOCK, one, 0)

    @pl.when(busy)
    def _():
        lane = lax.broadcasted_iota(jnp.int32, (HALF, TILE), 1)
        row = lax.broadcasted_iota(jnp.int32, (HALF, TILE), 0)
        for level in range(LEVELS):
            for c in range(2):
                tile = level * 16 + (row // BLOCK) * 4 + c * 2 + (row // TILE) % 2
                hot[level, c] = jnp.where(lane == tile, 1.0, 0.0).astype(jnp.bfloat16)
        mask_copy.wait()
        for t in range(8):
            q_tile = y * 16 + (t // 2) * 4 + core * 2 + t % 2
            allowed = mask[pl.ds(q_tile, 1), :]
            bias = jnp.where(allowed > 0, 0.0, MASKED)
            bias = jnp.concatenate([bias, jnp.zeros_like(bias)], axis=1)
            qa[pl.ds(t * TILE, TILE), pl.ds(HEAD_DIM, TILE)] = jnp.broadcast_to(
                bias, (TILE, TILE)
            ).astype(jnp.bfloat16)
        peak[...] = jnp.full(peak.shape, MASKED, jnp.float32)
        acc[...] = jnp.zeros(acc.shape, jnp.float32)

        for n in range(2):
            wait_pieces(n)
            y_copy(n, y, 0, 0, True).start()
            y_copy(n, y, 1, 0, False).start()
            y_copy(n, y, 1, 0, True).start()
            y_copy(n, y, 0, 0, False).start()
            sib_copy(n, 0, 0).start()
            sib_copy(n, 0, 1).start()
        wait_pieces(2)
        visit_all(0, core)

        def pass_on(n):
            y_copy(n, down, 0, 0, True).wait_recv()
            y_copy(n, down, 0, 1, True).start()
            sib_copy(n, 1, 0).start()
            y_copy(n, up, 1, 0, False).wait_recv()
            y_copy(n, up, 1, 1, False).start()
            sib_copy(n, 2, 1).start()
            y_copy(n, down, 1, 0, True).wait_recv()
            sib_copy(n, 1, 1).start()
            y_copy(n, up, 0, 0, False).wait_recv()
            sib_copy(n, 2, 0).start()

        def wait_sibling(step):
            for n in range(2):
                for half in range(2):
                    sib_copy(n, step, half, False).wait_recv()

        pass_on(0)
        wait_sibling(0)
        visit_all(0, 1 - core)
        pass_on(1)
        near_down, near_up = y != 0, y != 3

        @pl.when(near_down)
        def _():
            visit_all(1, core)

        @pl.when(near_up)
        def _():
            visit_all(2, core)

        wait_sibling(1)

        @pl.when(near_down)
        def _():
            visit_all(1, 1 - core)

        wait_sibling(2)

        @pl.when(near_up)
        def _():
            visit_all(2, 1 - core)

        far = (y + 2) % 4
        for n in range(2):
            y_copy(n, far, 0, 1, True).wait_recv()
            sib_copy(n, 3, 0).start()
            y_copy(n, far, 1, 1, False).wait_recv()
            sib_copy(n, 3, 1).start()
        visit_all(3, core)
        wait_sibling(3)

        def finish(q_block, _):
            visit(3, 1 - core, q_block)
            rows = pl.ds(pl.multiple_of(q_block * BLOCK, BLOCK), BLOCK)
            obuf[rows, :] = acc[rows, :HEAD_DIM] / acc[rows, HEAD_DIM:]

            def send_back(there, _):
                piece = q_block * 8 + there
                source = obuf.at[pl.ds(pl.multiple_of(piece * PIECE, PIECE), PIECE), :]
                target = out_ref.at[:, pl.ds(pl.multiple_of(me * HEAD_DIM, HEAD_DIM), HEAD_DIM)]
                mine = (q_block == zh) & (there == x * 2 + zl)

                @pl.when(jnp.logical_not(mine))
                def _():
                    pltpu.make_async_remote_copy(
                        src_ref=source, dst_ref=target, send_sem=o_send, recv_sem=o_recv,
                        device_id=(there, y * 8 + q_block * 2 + core), device_id_type=MESH,
                    ).start()

                @pl.when(mine)
                def _():
                    pltpu.make_async_copy(source, target, self_sem.at[3]).start()

                return 0

            lax.fori_loop(0, 8, send_back, 0)
            return 0

        lax.fori_loop(0, HALF // BLOCK, finish, 0)

        for n in range(2):
            for half in range(2):
                for way in (True, False):
                    y_copy(n, y, half, 0, way).wait_send()
                for step in range(4):
                    sib_copy(n, step, half).wait_send()
            y_copy(n, down, 0, 1, True).wait_send()
            y_copy(n, up, 1, 1, False).wait_send()
        sent = obuf.at[pl.ds(0, HALF - PIECE), :]
        pltpu.make_async_copy(sent, sent, o_send).wait()

    @pl.when(busy)
    def _():
        others = out_ref.at[:, pl.ds(0, (HEADS - 1) * HEAD_DIM)]
        one = out_ref.at[:, pl.ds(0, HEAD_DIM)]
        sent = q_ref.at[:, pl.ds(0, (HEADS - 1) * HEAD_DIM)]
        for n in range(3):
            pltpu.make_async_copy(sent, sent, in_send.at[n]).wait()
        pltpu.make_async_copy(one, one, self_sem.at[3]).wait()
        pltpu.make_async_copy(others, others, o_recv).wait()

    @pl.when(jnp.logical_not(busy))
    def _():
        for n in range(3):
            pltpu.make_async_copy(q_ref, q_ref, in_send.at[n]).wait()
        pltpu.make_async_copy(out_ref, out_ref, o_recv).wait()
        mask_copy.wait()


def local(queries, key_rows, values, tile_mask):
    bf16, f32, dma = jnp.bfloat16, jnp.float32, pltpu.SemaphoreType.DMA
    return pl.pallas_call(
        kernel,
        out_shape=jax.ShapeDtypeStruct(queries.shape, f32),
        in_specs=[pl.BlockSpec(memory_space=pltpu.HBM)] * 4,
        out_specs=pl.BlockSpec(memory_space=pltpu.VMEM),
        scratch_shapes=[
            pltpu.VMEM(tile_mask.shape, jnp.int32),
            pltpu.VMEM((HALF, 2 * HEAD_DIM), bf16),
            pltpu.VMEM((2, LEVELS, 2, HALF, HEAD_DIM), bf16),
            pltpu.VMEM((LEVELS, 2, HALF, TILE), bf16),
            pltpu.VMEM((HALF, HEAD_DIM), f32),
            pltpu.VMEM((HALF, 2 * HEAD_DIM), f32),
            pltpu.VMEM((HALF, HEAD_DIM), f32),
            dma((3,)),
            dma((3,)),
            dma((4,)),
            dma((2, 2, 2, 2)),
            dma((2, 2, 2, 2)),
            dma((2, 4, 2)),
            dma((2, 4, 2)),
            dma,
            dma,
            dma,
        ],
        compiler_params=pltpu.CompilerParams(
            collective_id=0, has_side_effects=True, vmem_limit_bytes=48 * 2**20
        ),
    )(queries, key_rows, values, tile_mask)


def solution(mesh):
    return jax.shard_map(
        local,
        mesh=mesh,
        in_specs=(
            P(("blk", "head"), None),
            P(("blk", "head"), None),
            P(("blk", "head"), None),
            P(),
        ),
        out_specs=P(("blk", "head"), None),
        check_vma=False,
    )
```

time: 693 us -> 73 us (0.11)
  the two profiles are of different devices: /device:TPU:16 before, /device:TPU:81 now
where the time goes in v1:
time: 73 us; the launch traced here: 72.8 us
  Pallas kernels  68.5 us (94%)
  local copies, waits for them, and re-layouts  4.28 us (6%)
    pallas_call x1, Pallas kernels, local(): pl.pallas_call(kernel, out_shape=jax.ShapeDtypeStruct(queries.shape, f32)...  68.5 us
    unnamed x9, local copies, waits for them, and re-layouts  4.28 us

profile of v1, /device:TPU:81, one launch (start us, length us, event | category | flops | bytes accessed | tf_op | source)
XLA Modules:
  0.0 72.8 jit_solution(361765392895642428)
XLA Ops:
  0.0 0.0 copy-start
  0.0 0.9 %copy-done = bf16[32,3072]{1,0:T(8,128)(2,1)S(1)} copy-done((bf16[32,3072]{1,0:T(8,128)(2,1)S(1)}, bf16[32,3072]{1,0:T(8,128)(2,1)}, u32[]{:S(2)}) %copy-start) | copy-done | bytes 196632
  0.9 0.0 copy-start.1
  0.9 0.9 %copy-done.1 = bf16[32,3072]{1,0:T(8,128)(2,1)S(1)} copy-done((bf16[32,3072]{1,0:T(8,128)(2,1)S(1)}, bf16[32,3072]{1,0:T(8,128)(2,1)}, u32[]{:S(2)}) %copy-start.1) | copy-done | bytes 196632
  1.9 0.0 copy-start.2
  1.9 0.9 %copy-done.2 = bf16[32,3072]{1,0:T(8,128)(2,1)S(1)} copy-done((bf16[32,3072]{1,0:T(8,128)(2,1)S(1)}, bf16[32,3072]{1,0:T(8,128)(2,1)}, u32[]{:S(2)}) %copy-start.2) | copy-done | bytes 196632
  2.8 0.0 copy-start.3
  2.8 0.8 %copy-done.3 = s32[64,64]{1,0:T(8,128)S(1)} copy-done((s32[64,64]{1,0:T(8,128)S(1)}, s32[64,64]{1,0:T(8,128)}, u32[]{:S(2)}) %copy-start.3) | copy-done | bytes 16408
  3.5 68.5 %shard_map.46 = f32[32,3072]{1,0:T(8,128)S(1)} custom-call(bf16[32,3072]{1,0:T(8,128)(2,1)S(1)} %copy-done, bf16[32,3072]{1,0:T(8,128)(2,1)S(1)} %copy-done.1, bf16[32,3072]{1,0:T(8,128)(2,1)S(1)} %copy-done.2, s32[64,64]{1,0:T(8,128)S(1)} %copy-done.3), custom_call_target="tpu_custom_call" | custom-call | tf_op jit(solution)/shard_map/pallas_call | solution.py:287
  72.1 0.7 %copy.6 = f32[32,3072]{1,0:T(8,128)} copy(f32[32,3072]{1,0:T(8,128)S(1)} %shard_map.46) | data formatting | bytes 786432
Async XLA Ops:
  0.0 0.9 %copy-start = (bf16[32,3072]{1,0:T(8,128)(2,1)S(1)}, bf16[32,3072]{1,0:T(8,128)(2,1)}, u32[]{:S(2)}) copy-start(bf16[32,3072]{1,0:T(8,128)(2,1)} %q_ref.1) | copy-start | bytes 589828
  0.9 0.9 %copy-start.1 = (bf16[32,3072]{1,0:T(8,128)(2,1)S(1)}, bf16[32,3072]{1,0:T(8,128)(2,1)}, u32[]{:S(2)}) copy-start(bf16[32,3072]{1,0:T(8,128)(2,1)} %k_ref.1) | copy-start | bytes 589828
  1.9 0.9 %copy-start.2 = (bf16[32,3072]{1,0:T(8,128)(2,1)S(1)}, bf16[32,3072]{1,0:T(8,128)(2,1)}, u32[]{:S(2)}) copy-start(bf16[32,3072]{1,0:T(8,128)(2,1)} %v_ref.1) | copy-start | bytes 589828
  2.8 0.8 %copy-start.3 = (s32[64,64]{1,0:T(8,128)S(1)}, s32[64,64]{1,0:T(8,128)}, u32[]{:S(2)}) copy-start(s32[64,64]{1,0:T(8,128)} %mask_ref.1) | copy-start | bytes 49156

commit v2 on v1

v2 whole, which is shorter than its diff:
```python
import jax
import jax.numpy as jnp
from jax import lax
from jax.experimental import pallas as pl
from jax.experimental.pallas import tpu as pltpu
from jax.sharding import PartitionSpec as P

MESH = pl.DeviceIdType.MESH

HEADS = 24
HEAD_DIM = 128
TILE = 128
PIECE = 32
LEVELS = 4
HALF = 1024
SLAB = 256
ORDER = (0, 1, 3, 2)
GOES_UP = (0, 3)
MASKED = -1e30
SCALE2 = HEAD_DIM**-0.5 * 1.4426950408889634


def place():
    head, blk = lax.axis_index("head"), lax.axis_index("blk")
    return head // 2, blk // 8, (blk // 2) % 4, head % 2, blk % 2


def column_of(head):
    return head // 8, head % 8


def device_at(x, y, z, core):
    return (x * 2 + z % 2, y * 8 + (z // 2) * 2 + core)


def span(r):
    return max(0, r - 2) * SLAB, (min(3, r + 2) + 1) * SLAB


def kernel(
    q_ref, k_ref, v_ref, mask_ref, out_ref,
    mask, qa, kv, wbuf, peaks, totals, gains, acc, obuf,
    in_sem, in_send, self_sem, y_recv, y_send, sib_recv, sib_send, o_recv, o_send, mask_sem,
):
    x, y, zh, zl, core = place()
    z = zh * 2 + zl
    me = x * 8 + z
    busy = x < 3
    slot = (zh * 8 + x * 2 + zl) * PIECE
    up, down, far = (y + 1) % 4, (y + 3) % 4, (y + 2) % 4
    levels = (y, down, up, far)
    sources = (k_ref, v_ref, q_ref)

    barrier = pltpu.get_barrier_semaphore()

    def greet(i, _):
        other = (me + i) % 32
        pl.semaphore_signal(
            barrier, inc=1, device_id=device_at(other // 8, y, other % 8, core), device_id_type=MESH
        )
        return 0

    lax.fori_loop(1, 32, greet, 0)
    for there in (
        device_at(x, up, z, core), device_at(x, down, z, core), device_at(x, y, z, 1 - core),
    ):
        pl.semaphore_signal(barrier, inc=1, device_id=there, device_id_type=MESH)
    with jax.named_scope("barrier"):
        pl.semaphore_wait(barrier, 34)

    def landing(n):
        if n == 2:
            return qa.at[pl.ds(slot, PIECE), pl.ds(0, HEAD_DIM)]
        return kv.at[n, y, core, pl.ds(slot, PIECE), :]

    def slab_rows(rel):
        return pl.ds(pl.multiple_of((zh + rel) % 4 * SLAB, SLAB), SLAB)

    def send_pieces(n):
        def send_piece(i, _):
            turn, w = i // 6, i % 6
            off = jnp.where(turn < 2, turn, 5 - turn)
            hz = (zh + off) % 4 * 2 + w % 2
            hx = (x + w // 2) % 3
            head = hx * 8 + hz
            source = sources[n].at[:, pl.ds(pl.multiple_of(head * HEAD_DIM, HEAD_DIM), HEAD_DIM)]

            @pl.when(head != me)
            def _():
                pltpu.make_async_remote_copy(
                    src_ref=source, dst_ref=landing(n), send_sem=in_send.at[n],
                    recv_sem=in_sem.at[n, (4 - off) % 4],
                    device_id=device_at(hx, y, hz, core), device_id_type=MESH,
                ).start()

            @pl.when(head == me)
            def _():
                pltpu.make_async_copy(source, landing(n), self_sem.at[n]).start()

            return 0

        lax.fori_loop(0, HEADS, send_piece, 0)

    with jax.named_scope("pieces out"):
        send_pieces(0)
        send_pieces(2)
        send_pieces(1)
    mask_copy = pltpu.make_async_copy(mask_ref, mask, mask_sem)
    mask_copy.start()

    def wait_slab(n, rel):
        if rel == 0:
            part = kv.at[0, 0, 0, pl.ds(0, SLAB - PIECE), :]
            pltpu.make_async_copy(part, part, in_sem.at[n, 0]).wait()
            pltpu.make_async_copy(landing(n), landing(n), self_sem.at[n]).wait()
        else:
            part = kv.at[0, 0, 0, pl.ds(0, SLAB), :]
            pltpu.make_async_copy(part, part, in_sem.at[n, rel]).wait()

    def y_copy(n, level, rel, step, up_way):
        part = kv.at[n, level, core, slab_rows(rel), :]
        return pltpu.make_async_remote_copy(
            src_ref=part, dst_ref=part, send_sem=y_send.at[n, step, rel, int(up_way)],
            recv_sem=y_recv.at[n, step, rel, int(up_way)],
            device_id=device_at(x, up if up_way else down, z, core), device_id_type=MESH,
        )

    def sib_copy(n, step, rel, from_me=True):
        whose = core if from_me else 1 - core
        part = kv.at[n, levels[step], whose, slab_rows(rel), :]
        return pltpu.make_async_remote_copy(
            src_ref=part, dst_ref=part, send_sem=sib_send.at[n, step, rel],
            recv_sem=sib_recv.at[n, step, rel],
            device_id=device_at(x, y, z, 1 - core), device_id_type=MESH,
        )

    def own_slab(n, rel):
        wait_slab(n, rel)
        y_copy(n, y, rel, 0, True).start()
        y_copy(n, y, rel, 0, False).start()
        sib_copy(n, 0, rel).start()

    def next_slab(n, rel):
        y_copy(n, down, rel, 0, True).wait_recv()
        if rel in GOES_UP:
            y_copy(n, down, rel, 1, True).start()
        sib_copy(n, 1, rel).start()
        y_copy(n, up, rel, 0, False).wait_recv()
        if rel not in GOES_UP:
            y_copy(n, up, rel, 1, False).start()
        sib_copy(n, 2, rel).start()

    def far_slab(n, rel):
        y_copy(n, far, rel, 1, rel in GOES_UP).wait_recv()
        sib_copy(n, 3, rel).start()

    def from_sibling(n, step):
        for rel in range(4):
            sib_copy(n, step, rel, False).wait_recv()

    def turn(i):
        step = i // 2
        off = jnp.where(step == 0, 0, jnp.where(step == 1, 3, jnp.where(step == 2, 1, 2)))
        return (y + off) % 4, (core + i) % 2

    def weigh(i, block=None):
        level, whose = turn(i)
        for r in range(4):
            lo, hi = span(r)
            rows = pl.ds(lo, hi - lo) if block is None else block
            lane = lax.broadcasted_iota(jnp.int32, (SLAB, TILE), 1)
            row = lax.broadcasted_iota(jnp.int32, (SLAB, TILE), 0)
            hot = lane == level * 16 + r * 4 + whose * 2 + row // TILE
            keys = jnp.concatenate(
                [
                    kv[0, level, whose, r * SLAB : (r + 1) * SLAB, :],
                    jnp.where(hot, 1.0, 0.0).astype(jnp.bfloat16),
                ],
                axis=1,
            )
            scores = lax.dot_general(
                qa[rows, :], keys, (((1,), (1,)), ((), ())), preferred_element_type=jnp.float32
            )
            peak = jnp.max(scores, axis=1, keepdims=True)
            weights = jnp.exp2((scores - peak) * SCALE2)
            wbuf[i, rows, r * SLAB : (r + 1) * SLAB] = weights.astype(jnp.bfloat16)
            before = peaks[rows, :]
            here = lax.broadcasted_iota(jnp.int32, before.shape, 1) == i * 4 + r
            peaks[rows, :] = jnp.where(here, peak, before)

    def mix(i, first=0, last=HALF):
        level, whose = turn(i)
        for r in range(4):
            lo, hi = max(span(r)[0], first), min(span(r)[1], last)
            if lo >= hi:
                continue
            rows = pl.ds(lo, hi - lo)
            lane = lax.broadcasted_iota(jnp.int32, (SLAB, TILE), 1)
            vals = jnp.concatenate(
                [
                    kv[1, level, whose, r * SLAB : (r + 1) * SLAB, :],
                    jnp.where(lane == i * 4 + r, 1.0, 0.0).astype(jnp.bfloat16),
                ],
                axis=1,
            )
            mixed = jnp.dot(
                wbuf[i, rows, r * SLAB : (r + 1) * SLAB], vals, preferred_element_type=jnp.float32
            )
            gain = gains[rows, :]
            here = lax.broadcasted_iota(jnp.int32, gain.shape, 1) == i * 4 + r
            gain = jnp.sum(jnp.where(here, gain, 0.0), axis=1, keepdims=True)
            acc[rows, :] += mixed[:, :HEAD_DIM] * gain
            totals[rows, :] += mixed[:, HEAD_DIM:]

    def near(i):
        level, _ = turn(i)
        return jnp.abs(level - y) < 3

    @pl.when(busy)
    def _():
        mask_copy.wait()
        for t in range(8):
            q_tile = y * 16 + (t // 2) * 4 + core * 2 + t % 2
            allowed = mask[pl.ds(q_tile, 1), :]
            bias = jnp.where(allowed > 0, 0.0, MASKED)
            bias = jnp.concatenate([bias, jnp.zeros_like(bias)], axis=1)
            qa[pl.ds(t * TILE, TILE), pl.ds(HEAD_DIM, TILE)] = jnp.broadcast_to(
                bias, (TILE, TILE)
            ).astype(jnp.bfloat16)
        peaks[...] = jnp.full(peaks.shape, MASKED, jnp.float32)
        totals[...] = jnp.zeros(totals.shape, jnp.float32)
        acc[...] = jnp.zeros(acc.shape, jnp.float32)

        with jax.named_scope("own keys"):
            own_slab(0, 0)
            own_slab(0, 1)
            own_slab(0, 3)
        with jax.named_scope("first next keys"):
            next_slab(0, 0)
            own_slab(0, 2)
        with jax.named_scope("next keys"):
            next_slab(0, 1)

        def weigh_own(k, _):
            for n, rel in enumerate(ORDER):

                @pl.when(k == n)
                def _(rel=rel):
                    with jax.named_scope("query slab"):
                        wait_slab(2, rel)

            @pl.when(k == 0)
            def _():
                with jax.named_scope("sibling keys"):
                    from_sibling(0, 0)

            @pl.when(k == 2)
            def _():
                with jax.named_scope("next keys"):
                    next_slab(0, 3)

            @pl.when(k == 3)
            def _():
                with jax.named_scope("next keys"):
                    next_slab(0, 2)

            rows = slab_rows(jnp.where(k < 2, k, 5 - k))
            with jax.named_scope("weigh own"):
                weigh(0, rows)
                weigh(1, rows)
            return 0

        lax.fori_loop(0, 4, weigh_own, 0)

        hooks = {
            2: (lambda: own_slab(1, 0),),
            3: (lambda: own_slab(1, 1), lambda: from_sibling(0, 1)),
            4: (lambda: own_slab(1, 3), lambda: far_slab(0, 0), lambda: far_slab(0, 1)),
            5: (lambda: own_slab(1, 2), lambda: next_slab(1, 0), lambda: from_sibling(0, 2)),
            6: (lambda: far_slab(0, 3), lambda: far_slab(0, 2), lambda: next_slab(1, 1)),
            7: (lambda: next_slab(1, 3), lambda: from_sibling(0, 3)),
        }

        def weigh_turn(i, _):
            for at, calls in hooks.items():

                @pl.when(i == at)
                def _(calls=calls):
                    with jax.named_scope("between weighings"):
                        for call in calls:
                            call()

            @pl.when(near(i))
            def _():
                with jax.named_scope("weigh"):
                    weigh(i)

            return 0

        lax.fori_loop(2, 8, weigh_turn, 0)
        every = peaks[...]
        gains[...] = jnp.exp2((every - jnp.max(every, axis=1, keepdims=True)) * SCALE2)

        mix_hooks = {
            0: (lambda: next_slab(1, 2),),
            1: (lambda: from_sibling(1, 0),),
            2: (lambda: far_slab(1, 0),),
            3: (lambda: far_slab(1, 1), lambda: from_sibling(1, 1)),
            4: (lambda: far_slab(1, 3),),
            5: (lambda: far_slab(1, 2), lambda: from_sibling(1, 2)),
        }

        def mix_turn(i, _):
            for at, calls in mix_hooks.items():

                @pl.when(i == at)
                def _(calls=calls):
                    with jax.named_scope("between mixings"):
                        for call in calls:
                            call()

            @pl.when(near(i))
            def _():
                with jax.named_scope("mix"):
                    mix(i)

            return 0

        lax.fori_loop(0, 6, mix_turn, 0)
        with jax.named_scope("last sibling values"):
            from_sibling(1, 3)

        for q_block in range(HALF // SLAB):
            rows = pl.ds(q_block * SLAB, SLAB)
            with jax.named_scope("last mix"):
                for i in (6, 7):
                    mix(i, q_block * SLAB, (q_block + 1) * SLAB)
                total = jnp.sum(totals[rows, :] * gains[rows, :], axis=1, keepdims=True)
                obuf[rows, :] = (acc[rows, :] / total).astype(jnp.bfloat16)

            def send_back(there, _, q_block=q_block):
                piece = q_block * 8 + there
                source = obuf.at[pl.ds(pl.multiple_of(piece * PIECE, PIECE), PIECE), :]
                target = out_ref.at[:, pl.ds(pl.multiple_of(me * HEAD_DIM, HEAD_DIM), HEAD_DIM)]
                mine = (q_block == zh) & (there == x * 2 + zl)

                @pl.when(jnp.logical_not(mine))
                def _():
                    pltpu.make_async_remote_copy(
                        src_ref=source, dst_ref=target, send_sem=o_send, recv_sem=o_recv,
                        device_id=(there, y * 8 + q_block * 2 + core), device_id_type=MESH,
                    ).start()

                @pl.when(mine)
                def _():
                    pltpu.make_async_copy(source, target, self_sem.at[3]).start()

                return 0

            lax.fori_loop(0, 8, send_back, 0)

        for n in range(2):
            for rel in range(4):
                for way in (True, False):
                    y_copy(n, y, rel, 0, way).wait_send()
                for step in range(4):
                    sib_copy(n, step, rel).wait_send()
                if rel in GOES_UP:
                    y_copy(n, down, rel, 1, True).wait_send()
                else:
                    y_copy(n, up, rel, 1, False).wait_send()
        others = out_ref.at[:, pl.ds(0, (HEADS - 1) * HEAD_DIM)]
        for n in range(3):
            pltpu.make_async_copy(others, others, in_send.at[n]).wait()
        sent = obuf.at[pl.ds(0, HALF - PIECE), :]
        with jax.named_scope("output sent"):
            pltpu.make_async_copy(sent, sent, o_send).wait()
        one = out_ref.at[:, pl.ds(0, HEAD_DIM)]
        pltpu.make_async_copy(one, one, self_sem.at[3]).wait()
        with jax.named_scope("output here"):
            pltpu.make_async_copy(others, others, o_recv).wait()

    @pl.when(jnp.logical_not(busy))
    def _():
        mask_copy.wait()
        for n in range(3):
            pltpu.make_async_copy(out_ref, out_ref, in_send.at[n]).wait()
        pltpu.make_async_copy(out_ref, out_ref, o_recv).wait()


def local(queries, key_rows, values, tile_mask):
    bf16, f32, dma = jnp.bfloat16, jnp.float32, pltpu.SemaphoreType.DMA
    queries, key_rows, values, tile_mask = (
        pltpu.with_memory_space_constraint(a, pltpu.HBM) for a in (queries, key_rows, values, tile_mask)
    )
    gathered = pl.pallas_call(
        kernel,
        out_shape=jax.ShapeDtypeStruct(queries.shape, bf16),
        in_specs=[pl.BlockSpec(memory_space=pltpu.HBM)] * 4,
        out_specs=pl.BlockSpec(memory_space=pltpu.VMEM),
        scratch_shapes=[
            pltpu.VMEM(tile_mask.shape, jnp.int32),
            pltpu.VMEM((HALF, 2 * HEAD_DIM), bf16),
            pltpu.VMEM((2, LEVELS, 2, HALF, HEAD_DIM), bf16),
            pltpu.VMEM((8, HALF, HALF), bf16),
            pltpu.VMEM((HALF, TILE), f32),
            pltpu.VMEM((HALF, TILE), f32),
            pltpu.VMEM((HALF, TILE), f32),
            pltpu.VMEM((HALF, HEAD_DIM), f32),
            pltpu.VMEM((HALF, HEAD_DIM), bf16),
            dma((3, 4)),
            dma((3,)),
            dma((4,)),
            dma((2, 2, 4, 2)),
            dma((2, 2, 4, 2)),
            dma((2, 4, 4)),
            dma((2, 4, 4)),
            dma,
            dma,
            dma,
        ],
        compiler_params=pltpu.CompilerParams(
            collective_id=0, has_side_effects=True, vmem_limit_bytes=48 * 2**20
        ),
    )(queries, key_rows, values, tile_mask)
    return gathered.astype(f32)


def solution(mesh):
    return jax.shard_map(
        local,
        mesh=mesh,
        in_specs=(
            P(("blk", "head"), None),
            P(("blk", "head"), None),
            P(("blk", "head"), None),
            P(),
        ),
        out_specs=P(("blk", "head"), None),
        check_vma=False,
    )
```

time: 73 us -> 49.9 us (0.68)
  the two profiles are of different devices: /device:TPU:81 before, /device:TPU:64 now
where the time goes in v2:
time: 49.9 us; the launch traced here: 49.6 us
  Pallas kernels  48.8 us (98%)
  other arithmetic  0.77 us (2%)
    pallas_call x1, Pallas kernels, local(): pl.pallas_call(kernel, out_shape=jax.ShapeDtypeStruct(queries.shape, bf16...  48.8 us

profile of v2, /device:TPU:64, one launch (start us, length us, event | category | flops | bytes accessed | tf_op | source)
XLA Modules:
  0.0 49.6 jit_solution(12246447217751751808)
XLA Ops:
  0.0 48.8 %shard_map.46 = bf16[32,3072]{1,0:T(8,128)(2,1)S(1)} custom-call(bf16[32,3072]{1,0:T(8,128)(2,1)} %q_ref.1, bf16[32,3072]{1,0:T(8,128)(2,1)} %k_ref.1, bf16[32,3072]{1,0:T(8,128)(2,1)} %v_ref.1, s32[64,64]{1,0:T(8,128)} %mask_ref.1), custom_call_target="tpu_custom_call" | custom-call | tf_op jit(solution)/shard_map/pallas_call | solution.py:396
  48.8 0.8 %convert_element_type.3 = f32[32,3072]{1,0:T(8,128)} convert(bf16[32,3072]{1,0:T(8,128)(2,1)S(1)} %shard_map.46) | non-fusion elementwise | flops 98304 | bytes 589824 | tf_op jit(solution)/shard_map/convert_element_type | solution.py:426

commit v3 on v2

v3 whole, which is shorter than its diff:
```python
import jax
import jax.numpy as jnp
from jax import lax
from jax.experimental import pallas as pl
from jax.experimental.pallas import tpu as pltpu
from jax.sharding import PartitionSpec as P

MESH = pl.DeviceIdType.MESH

HEADS = 24
HEAD_DIM = 128
TILE = 128
PIECE = 32
LEVELS = 4
HALF = 1024
SLAB = 256
ORDER = (0, 1, 3, 2)
GOES_UP = (0, 3)
MASKED = -1e30
SCALE2 = HEAD_DIM**-0.5 * 1.4426950408889634


def place():
    head, blk = lax.axis_index("head"), lax.axis_index("blk")
    return head // 2, blk // 8, (blk // 2) % 4, head % 2, blk % 2


def column_of(head):
    return head // 8, head % 8


def device_at(x, y, z, core):
    return (x * 2 + z % 2, y * 8 + (z // 2) * 2 + core)


def span(r):
    return max(0, r - 2) * SLAB, (min(3, r + 2) + 1) * SLAB


def kernel(
    q_ref, k_ref, v_ref, mask_ref, out_ref,
    mask, rows_in, qa, kv, wbuf, peaks, totals, gains, acc, obuf,
    in_sem, in_send, self_sem, y_recv, y_send, sib_recv, sib_send, o_recv, o_send, mask_sem, load_sem,
):
    x, y, zh, zl, core = place()
    z = zh * 2 + zl
    me = x * 8 + z
    busy = x < 3
    slot = (zh * 8 + x * 2 + zl) * PIECE
    up, down, far = (y + 1) % 4, (y + 3) % 4, (y + 2) % 4
    levels = (y, down, up, far)
    sources = (rows_in.at[0], rows_in.at[1], rows_in.at[2])
    loads = [
        pltpu.make_async_copy(ref, rows_in.at[n], load_sem.at[n])
        for n, ref in enumerate((k_ref, v_ref, q_ref))
    ]
    for n in (0, 2, 1):
        loads[n].start()

    mask_copy = pltpu.make_async_copy(mask_ref, mask, mask_sem)
    mask_copy.start()
    barrier = pltpu.get_barrier_semaphore()

    def greet(i, _):
        hx, hz = i // 8, (z + i) % 8

        @pl.when((hx * 8 + hz != me) & (busy | (hx < 3)))
        def _():
            pl.semaphore_signal(
                barrier, inc=1, device_id=device_at(hx, y, hz, core), device_id_type=MESH
            )

        return 0

    lax.fori_loop(0, 32, greet, 0)

    @pl.when(busy)
    def _():
        for there in (
            device_at(x, up, z, core), device_at(x, down, z, core), device_at(x, y, z, 1 - core),
        ):
            pl.semaphore_signal(barrier, inc=1, device_id=there, device_id_type=MESH)

    @pl.when(busy)
    def _():
        mask_copy.wait()
        for t in range(8):
            q_tile = y * 16 + (t // 2) * 4 + core * 2 + t % 2
            allowed = mask[pl.ds(q_tile, 1), :]
            bias = jnp.where(allowed > 0, 0.0, MASKED)
            bias = jnp.concatenate([bias, jnp.zeros_like(bias)], axis=1)
            qa[pl.ds(t * TILE, TILE), pl.ds(HEAD_DIM, TILE)] = jnp.broadcast_to(
                bias, (TILE, TILE)
            ).astype(jnp.bfloat16)
        peaks[...] = jnp.full(peaks.shape, MASKED, jnp.float32)
        totals[...] = jnp.zeros(totals.shape, jnp.float32)
        acc[...] = jnp.zeros(acc.shape, jnp.float32)

        wbuf[7, pl.ds(0, SLAB), pl.ds(3 * SLAB, SLAB)] = jnp.zeros((SLAB, SLAB), jnp.bfloat16)
        wbuf[7, pl.ds(3 * SLAB, SLAB), pl.ds(0, SLAB)] = jnp.zeros((SLAB, SLAB), jnp.bfloat16)

    with jax.named_scope("barrier"):
        @pl.when(busy)
        def _():
            pl.semaphore_wait(barrier, 34)

        @pl.when(jnp.logical_not(busy))
        def _():
            pl.semaphore_wait(barrier, HEADS)


    def landing(n):
        if n == 2:
            return qa.at[pl.ds(slot, PIECE), pl.ds(0, HEAD_DIM)]
        return kv.at[n, y, core, pl.ds(slot, PIECE), :]

    def slab_rows(rel):
        return pl.ds(pl.multiple_of((zh + rel) % 4 * SLAB, SLAB), SLAB)

    def send_pieces(n):
        def send_piece(i, _):
            turn, w = i // 6, i % 6
            off = jnp.where(turn < 2, turn, 5 - turn)
            hz = (zh + off) % 4 * 2 + w % 2
            hx = (x + w // 2) % 3
            head = hx * 8 + hz
            source = sources[n].at[:, pl.ds(pl.multiple_of(head * HEAD_DIM, HEAD_DIM), HEAD_DIM)]

            @pl.when(head != me)
            def _():
                pltpu.make_async_remote_copy(
                    src_ref=source, dst_ref=landing(n), send_sem=in_send.at[n],
                    recv_sem=in_sem.at[n, (4 - off) % 4],
                    device_id=device_at(hx, y, hz, core), device_id_type=MESH,
                ).start()

            @pl.when(head == me)
            def _():
                pltpu.make_async_copy(source, landing(n), self_sem.at[n]).start()

            return 0

        lax.fori_loop(0, HEADS, send_piece, 0)

    with jax.named_scope("pieces out"):
        for n in (0, 2, 1):
            loads[n].wait()
            send_pieces(n)

    def wait_slab(n, rel):
        if rel == 0:
            part = kv.at[0, 0, 0, pl.ds(0, SLAB - PIECE), :]
            pltpu.make_async_copy(part, part, in_sem.at[n, 0]).wait()
            pltpu.make_async_copy(landing(n), landing(n), self_sem.at[n]).wait()
        else:
            part = kv.at[0, 0, 0, pl.ds(0, SLAB), :]
            pltpu.make_async_copy(part, part, in_sem.at[n, rel]).wait()

    def y_copy(n, level, rel, way):
        part = kv.at[n, level, core, slab_rows(rel), :]
        upward = rel in GOES_UP if way == 2 else way == 0
        return pltpu.make_async_remote_copy(
            src_ref=part, dst_ref=part, send_sem=y_send, recv_sem=y_recv.at[n, way, rel],
            device_id=device_at(x, up if upward else down, z, core), device_id_type=MESH,
        )

    def to_sibling(n, step, rel=None):
        part = kv.at[n, levels[step], core]
        if rel is not None:
            part = part.at[slab_rows(rel), :]
        pltpu.make_async_remote_copy(
            src_ref=part, dst_ref=part, send_sem=sib_send, recv_sem=sib_recv.at[n, step],
            device_id=device_at(x, y, z, 1 - core), device_id_type=MESH,
        ).start()

    def own_slab(n, rel):
        wait_slab(n, rel)
        y_copy(n, y, rel, 0).start()
        y_copy(n, y, rel, 1).start()
        if rel == ORDER[-1]:
            to_sibling(n, 0)

    def next_slab(n, rel):
        y_copy(n, down, rel, 0).wait_recv()
        if rel in GOES_UP:
            y_copy(n, down, rel, 2).start()
        y_copy(n, up, rel, 1).wait_recv()
        if rel not in GOES_UP:
            y_copy(n, up, rel, 2).start()
        if rel == ORDER[-1]:
            to_sibling(n, 1)
            to_sibling(n, 2)

    def far_slab(n, rel):
        y_copy(n, far, rel, 2).wait_recv()
        if n == 1:
            to_sibling(n, 3, rel)
        elif rel == ORDER[-1]:
            to_sibling(n, 3)

    def from_sibling(n, step):
        part = kv.at[n, levels[step], 1 - core]
        pltpu.make_async_copy(part, part, sib_recv.at[n, step]).wait()

    def turn(i):
        step = i // 2
        off = jnp.where(step == 0, 0, jnp.where(step == 1, 3, jnp.where(step == 2, 1, 2)))
        return (y + off) % 4, (core + i) % 2

    def weigh(i, block=None):
        level, whose = turn(i)
        for r in range(4):
            lo, hi = span(r)
            rows = pl.ds(lo, hi - lo) if block is None else block
            lane = lax.broadcasted_iota(jnp.int32, (SLAB, TILE), 1)
            row = lax.broadcasted_iota(jnp.int32, (SLAB, TILE), 0)
            hot = lane == level * 16 + r * 4 + whose * 2 + row // TILE
            keys = jnp.concatenate(
                [
                    kv[0, level, whose, r * SLAB : (r + 1) * SLAB, :],
                    jnp.where(hot, 1.0, 0.0).astype(jnp.bfloat16),
                ],
                axis=1,
            )
            scores = lax.dot_general(
                qa[rows, :], keys, (((1,), (1,)), ((), ())), preferred_element_type=jnp.float32
            )
            peak = jnp.max(scores, axis=1, keepdims=True)
            weights = jnp.exp2((scores - peak) * SCALE2)
            wbuf[i, rows, r * SLAB : (r + 1) * SLAB] = weights.astype(jnp.bfloat16)
            before = peaks[rows, :]
            here = lax.broadcasted_iota(jnp.int32, before.shape, 1) == i * 4 + r
            peaks[rows, :] = jnp.where(here, peak, before)

    def mix(i, block=None):
        level, whose = turn(i)
        for r in range(4):
            lo, hi = span(r)
            rows = pl.ds(lo, hi - lo) if block is None else block
            lane = lax.broadcasted_iota(jnp.int32, (SLAB, TILE), 1)
            vals = jnp.concatenate(
                [
                    kv[1, level, whose, r * SLAB : (r + 1) * SLAB, :],
                    jnp.where(lane == i * 4 + r, 1.0, 0.0).astype(jnp.bfloat16),
                ],
                axis=1,
            )
            mixed = jnp.dot(
                wbuf[i, rows, r * SLAB : (r + 1) * SLAB], vals, preferred_element_type=jnp.float32
            )
            gain = gains[rows, :]
            here = lax.broadcasted_iota(jnp.int32, gain.shape, 1) == i * 4 + r
            gain = jnp.sum(jnp.where(here, gain, 0.0), axis=1, keepdims=True)
            acc[rows, :] += mixed[:, :HEAD_DIM] * gain
            totals[rows, :] += mixed[:, HEAD_DIM:]

    def near(i):
        level, _ = turn(i)
        return jnp.abs(level - y) < 3

    @pl.when(busy)
    def _():
        own_slab(0, 0)
        own_slab(0, 1)
        own_slab(0, 3)
        own_slab(0, 2)
        next_slab(0, 0)
        next_slab(0, 1)

        def run_hooks(hooks, i):
            if isinstance(i, int):
                for call, n, which in hooks.get(i, ()):
                    call(n, which)
                return
            for at, calls in hooks.items():

                @pl.when(i == at)
                def _(calls=calls):
                    for call, n, which in calls:
                        call(n, which)

        own_hooks = {
            0: ((wait_slab, 2, 0), (wait_slab, 2, 1)),
            1: ((next_slab, 0, 3), (from_sibling, 0, 0)),
            2: ((next_slab, 0, 2), (wait_slab, 2, 3), (wait_slab, 2, 2)),
            3: ((own_slab, 1, 0),),
        }

        def weigh_own(j, _):
            run_hooks(own_hooks, j)
            with jax.named_scope("weigh own"):
                for k in range(2):
                    weigh(j % 2, slab_rows(jnp.where(j < 2, k, 3 - k)))
            return 0

        lax.fori_loop(0, 4, weigh_own, 0)

        weigh_hooks = {
            2: ((own_slab, 1, 1),),
            3: ((own_slab, 1, 3), (from_sibling, 0, 1)),
            4: ((own_slab, 1, 2), (far_slab, 0, 0), (far_slab, 0, 1), (far_slab, 0, 3), (far_slab, 0, 2)),
            5: ((from_sibling, 0, 2),),
            6: ((next_slab, 1, 0),),
            7: ((next_slab, 1, 1), (from_sibling, 0, 3)),
        }
        mix_hooks = {
            0: ((next_slab, 1, 3),),
            1: ((next_slab, 1, 2), (from_sibling, 1, 0)),
            3: ((far_slab, 1, 0),),
            4: ((far_slab, 1, 1), (from_sibling, 1, 1)),
            5: ((from_sibling, 1, 2), (far_slab, 1, 3)),
            6: ((far_slab, 1, 2),),
        }

        def weigh_turn(i, _):
            run_hooks(weigh_hooks, i)

            def _():
                with jax.named_scope("weigh"):
                    weigh(i)

            _() if i > 5 else pl.when(near(i))(_)

            return 0

        for i in range(2, 8):
            weigh_turn(i, 0)
        every = peaks[...]
        gains[...] = jnp.exp2((every - jnp.max(every, axis=1, keepdims=True)) * SCALE2)

        def mix_turn(m, _):
            run_hooks(mix_hooks, m)
            i = (0, 1, 2, 4, 3, 5, 6)[m]

            def _():
                with jax.named_scope("mix"):
                    mix(i)

            _() if i > 5 or i < 2 else pl.when(near(i))(_)

            return 0

        for m in range(7):
            mix_turn(m, 0)
        from_sibling(1, 3)

        def finish(q_block, _):
            rows = pl.ds(pl.multiple_of(q_block * SLAB, SLAB), SLAB)
            with jax.named_scope("last mix"):
                mix(7, rows)
                total = jnp.sum(totals[rows, :] * gains[rows, :], axis=1, keepdims=True)
                obuf[rows, :] = (acc[rows, :] / total).astype(jnp.bfloat16)

            def send_back(there, _):
                piece = q_block * 8 + there
                source = obuf.at[pl.ds(pl.multiple_of(piece * PIECE, PIECE), PIECE), :]
                target = out_ref.at[:, pl.ds(pl.multiple_of(me * HEAD_DIM, HEAD_DIM), HEAD_DIM)]
                mine = (q_block == zh) & (there == x * 2 + zl)

                @pl.when(jnp.logical_not(mine))
                def _():
                    pltpu.make_async_remote_copy(
                        src_ref=source, dst_ref=target, send_sem=o_send, recv_sem=o_recv,
                        device_id=(there, y * 8 + q_block * 2 + core), device_id_type=MESH,
                    ).start()

                @pl.when(mine)
                def _():
                    pltpu.make_async_copy(source, target, self_sem.at[3]).start()

                return 0

            lax.fori_loop(0, 8, send_back, 0)
            return 0

        lax.fori_loop(0, 4, finish, 0)

        gone = kv.at[0, pl.ds(0, 3)]
        pltpu.make_async_copy(gone, gone, y_send).wait()
        pltpu.make_async_copy(kv.at[0], kv.at[0], sib_send).wait()
        others = out_ref.at[:, pl.ds(0, (HEADS - 1) * HEAD_DIM)]
        for n in range(3):
            pltpu.make_async_copy(others, others, in_send.at[n]).wait()
        sent = obuf.at[pl.ds(0, HALF - PIECE), :]
        with jax.named_scope("output sent"):
            pltpu.make_async_copy(sent, sent, o_send).wait()
        one = out_ref.at[:, pl.ds(0, HEAD_DIM)]
        pltpu.make_async_copy(one, one, self_sem.at[3]).wait()
        with jax.named_scope("output here"):
            pltpu.make_async_copy(others, others, o_recv).wait()

    @pl.when(jnp.logical_not(busy))
    def _():
        mask_copy.wait()
        for n in range(3):
            pltpu.make_async_copy(out_ref, out_ref, in_send.at[n]).wait()
        pltpu.make_async_copy(out_ref, out_ref, o_recv).wait()


def local(queries, key_rows, values, tile_mask):
    bf16, f32, dma = jnp.bfloat16, jnp.float32, pltpu.SemaphoreType.DMA
    queries, key_rows, values, tile_mask = (
        pltpu.with_memory_space_constraint(a, pltpu.HBM) for a in (queries, key_rows, values, tile_mask)
    )
    gathered = pl.pallas_call(
        kernel,
        out_shape=jax.ShapeDtypeStruct(queries.shape, bf16),
        in_specs=[pl.BlockSpec(memory_space=pltpu.HBM)] * 4,
        out_specs=pl.BlockSpec(memory_space=pltpu.VMEM),
        scratch_shapes=[
            pltpu.VMEM(tile_mask.shape, jnp.int32),
            pltpu.VMEM((3, *queries.shape), bf16),
            pltpu.VMEM((HALF, 2 * HEAD_DIM), bf16),
            pltpu.VMEM((2, LEVELS, 2, HALF, HEAD_DIM), bf16),
            pltpu.VMEM((8, HALF, HALF), bf16),
            pltpu.VMEM((HALF, TILE), f32),
            pltpu.VMEM((HALF, TILE), f32),
            pltpu.VMEM((HALF, TILE), f32),
            pltpu.VMEM((HALF, HEAD_DIM), f32),
            pltpu.VMEM((HALF, HEAD_DIM), bf16),
            dma((3, 4)),
            dma((3,)),
            dma((4,)),
            dma((2, 3, 4)),
            dma,
            dma((2, 4)),
            dma,
            dma,
            dma,
            dma,
            dma((3,)),
        ],
        compiler_params=pltpu.CompilerParams(
            collective_id=0, has_side_effects=True, vmem_limit_bytes=48 * 2**20
        ),
    )(queries, key_rows, values, tile_mask)
    return gathered.astype(f32)


def solution(mesh):
    return jax.shard_map(
        local,
        mesh=mesh,
        in_specs=(
            P(("blk", "head"), None),
            P(("blk", "head"), None),
            P(("blk", "head"), None),
            P(),
        ),
        out_specs=P(("blk", "head"), None),
        check_vma=False,
    )
```

time: 49.9 us -> 47.8 us (0.958)
  Pallas kernels: 48.8 us -> 46.9 us
    pallas_call x1, Pallas kernels: 48.8 us -> 46.9 us  [local(): pl.pallas_call(kernel, out_shape=jax.ShapeDtypeStruct(queries.shape, bf16...]
where the time goes in v3:
time: 47.8 us; the launch traced here: 47.7 us
  Pallas kernels  46.9 us (98%)
  other arithmetic  0.77 us (2%)
    pallas_call x1, Pallas kernels, local(): pl.pallas_call(kernel, out_shape=jax.ShapeDtypeStruct(queries.shape, bf16...  46.9 us

profile of v3, /device:TPU:64, one launch (start us, length us, event | category | flops | bytes accessed | tf_op | source)
XLA Modules:
  0.0 47.7 jit_solution(13951909277569279517)
XLA Ops:
  0.0 46.9 %shard_map.46 = bf16[32,3072]{1,0:T(8,128)(2,1)S(1)} custom-call(bf16[32,3072]{1,0:T(8,128)(2,1)} %q_ref.1, bf16[32,3072]{1,0:T(8,128)(2,1)} %k_ref.1, bf16[32,3072]{1,0:T(8,128)(2,1)} %v_ref.1, s32[64,64]{1,0:T(8,128)} %mask_ref.1), custom_call_target="tpu_custom_call" | custom-call | tf_op jit(solution)/shard_map/pallas_call | solution.py:405
  47.0 0.8 %convert_element_type.3 = f32[32,3072]{1,0:T(8,128)} convert(bf16[32,3072]{1,0:T(8,128)(2,1)S(1)} %shard_map.46) | non-fusion elementwise | flops 98304 | bytes 589824 | tf_op jit(solution)/shard_map/convert_element_type | solution.py:437

commit v4 on v3

--- a/solution.py
+++ b/solution.py
@@ -50,6 +50,31 @@
     up, down, far = (y + 1) % 4, (y + 3) % 4, (y + 2) % 4
     levels = (y, down, up, far)
     sources = (rows_in.at[0], rows_in.at[1], rows_in.at[2])
+    barrier = pltpu.get_barrier_semaphore()
+
+    def greet(i, _):
+        turn = i // 4
+        far_off = (turn + 1) // 2
+        hz = jnp.where(turn % 2 == 1, z + 4 - far_off, z + 4 + far_off) % 8
+        hx = (x + 2 + i) % 4
+
+        @pl.when((hx * 8 + hz != me) & (busy | (hx < 3)))
+        def _():
+            pl.semaphore_signal(
+                barrier, inc=1, device_id=device_at(hx, y, hz, core), device_id_type=MESH
+            )
+
+        return 0
+
+    lax.fori_loop(0, 32, greet, 0)
+
+    @pl.when(busy)
+    def _():
+        for there in (
+            device_at(x, up, z, core), device_at(x, down, z, core), device_at(x, y, z, 1 - core),
+        ):
+            pl.semaphore_signal(barrier, inc=1, device_id=there, device_id_type=MESH)
+
     loads = [
         pltpu.make_async_copy(ref, rows_in.at[n], load_sem.at[n])
         for n, ref in enumerate((k_ref, v_ref, q_ref))
@@ -59,28 +84,6 @@
 
     mask_copy = pltpu.make_async_copy(mask_ref, mask, mask_sem)
     mask_copy.start()
-    barrier = pltpu.get_barrier_semaphore()
-
-    def greet(i, _):
-        hx, hz = i // 8, (z + i) % 8
-
-        @pl.when((hx * 8 + hz != me) & (busy | (hx < 3)))
-        def _():
-            pl.semaphore_signal(
-                barrier, inc=1, device_id=device_at(hx, y, hz, core), device_id_type=MESH
-            )
-
-        return 0
-
-    lax.fori_loop(0, 32, greet, 0)
-
-    @pl.when(busy)
-    def _():
-        for there in (
-            device_at(x, up, z, core), device_at(x, down, z, core), device_at(x, y, z, 1 - core),
-        ):
-            pl.semaphore_signal(barrier, inc=1, device_id=there, device_id_type=MESH)
-
     @pl.when(busy)
     def _():
         mask_copy.wait()
@@ -279,21 +282,23 @@
                     for call, n, which in calls:
                         call(n, which)
 
-        own_hooks = {
-            0: ((wait_slab, 2, 0), (wait_slab, 2, 1)),
-            1: ((next_slab, 0, 3), (from_sibling, 0, 0)),
-            2: ((next_slab, 0, 2), (wait_slab, 2, 3), (wait_slab, 2, 2)),
-            3: ((own_slab, 1, 0),),
-        }
-
-        def weigh_own(j, _):
-            run_hooks(own_hooks, j)
+        def weigh_own(pair, turns):
             with jax.named_scope("weigh own"):
-                for k in range(2):
-                    weigh(j % 2, slab_rows(jnp.where(j < 2, k, 3 - k)))
-            return 0
-
-        lax.fori_loop(0, 4, weigh_own, 0)
+                for i in turns:
+                    for rel in pair:
+                        weigh(i, slab_rows(rel))
+
+        wait_slab(2, 0)
+        wait_slab(2, 1)
+        weigh_own((0, 1), (0,))
+        next_slab(0, 3)
+        from_sibling(0, 0)
+        weigh_own((0, 1), (1,))
+        next_slab(0, 2)
+        wait_slab(2, 3)
+        wait_slab(2, 2)
+        own_slab(1, 0)
+        weigh_own((3, 2), (0, 1))
 
         weigh_hooks = {
             2: ((own_slab, 1, 1),),
@@ -304,12 +309,10 @@
             7: ((next_slab, 1, 1), (from_sibling, 0, 3)),
         }
         mix_hooks = {
-            0: ((next_slab, 1, 3),),
-            1: ((next_slab, 1, 2), (from_sibling, 1, 0)),
+            0: ((next_slab, 1, 3), (next_slab, 1, 2), (from_sibling, 1, 0)),
             3: ((far_slab, 1, 0),),
             4: ((far_slab, 1, 1), (from_sibling, 1, 1)),
-            5: ((from_sibling, 1, 2), (far_slab, 1, 3)),
-            6: ((far_slab, 1, 2),),
+            5: ((from_sibling, 1, 2), (far_slab, 1, 3), (far_slab, 1, 2)),
         }
 
         def weigh_turn(i, _):
@@ -340,7 +343,11 @@
 
             return 0
 
-        for m in range(7):
+        run_hooks(mix_hooks, 0)
+        with jax.named_scope("mix"):
+            mix(0)
+            mix(1)
+        for m in range(2, 7):
             mix_turn(m, 0)
         from_sibling(1, 3)
 
@@ -351,7 +358,8 @@
                 total = jnp.sum(totals[rows, :] * gains[rows, :], axis=1, keepdims=True)
                 obuf[rows, :] = (acc[rows, :] / total).astype(jnp.bfloat16)
 
-            def send_back(there, _):
+            def send_back(i, _):
+                there = (i + x * 2 + zl) % 8
                 piece = q_block * 8 + there
                 source = obuf.at[pl.ds(pl.multiple_of(piece * PIECE, PIECE), PIECE), :]
                 target = out_ref.at[:, pl.ds(pl.multiple_of(me * HEAD_DIM, HEAD_DIM), HEAD_DIM)]

time: 47.8 us -> 47.6 us (level)
  no operation moved by 1% of the time
where the time goes in v4:
time: 47.6 us; the launch traced here: 47.5 us
  Pallas kernels  46.7 us (98%)
  other arithmetic  0.77 us (2%)
    pallas_call x1, Pallas kernels, local(): pl.pallas_call(kernel, out_shape=jax.ShapeDtypeStruct(queries.shape, bf16...  46.7 us

profile of v4, /device:TPU:64, one launch (start us, length us, event | category | flops | bytes accessed | tf_op | source)
XLA Modules:
  0.0 47.5 jit_solution(14173375242333889574)
XLA Ops:
  0.0 46.7 %shard_map.46 = bf16[32,3072]{1,0:T(8,128)(2,1)S(1)} custom-call(bf16[32,3072]{1,0:T(8,128)(2,1)} %q_ref.1, bf16[32,3072]{1,0:T(8,128)(2,1)} %k_ref.1, bf16[32,3072]{1,0:T(8,128)(2,1)} %v_ref.1, s32[64,64]{1,0:T(8,128)} %mask_ref.1), custom_call_target="tpu_custom_call" | custom-call | tf_op jit(solution)/shard_map/pallas_call | solution.py:413
  46.8 0.8 %convert_element_type.3 = f32[32,3072]{1,0:T(8,128)} convert(bf16[32,3072]{1,0:T(8,128)(2,1)S(1)} %shard_map.46) | non-fusion elementwise | flops 98304 | bytes 589824 | tf_op jit(solution)/shard_map/convert_element_type | solution.py:445

commit v5 on v3

--- a/solution.py
+++ b/solution.py
@@ -50,6 +50,31 @@
     up, down, far = (y + 1) % 4, (y + 3) % 4, (y + 2) % 4
     levels = (y, down, up, far)
     sources = (rows_in.at[0], rows_in.at[1], rows_in.at[2])
+    barrier = pltpu.get_barrier_semaphore()
+
+    def greet(i, _):
+        turn = i // 4
+        far_off = (turn + 1) // 2
+        hz = jnp.where(turn % 2 == 1, z + 4 - far_off, z + 4 + far_off) % 8
+        hx = (x + 2 + i) % 4
+
+        @pl.when((hx * 8 + hz != me) & (busy | (hx < 3)))
+        def _():
+            pl.semaphore_signal(
+                barrier, inc=1, device_id=device_at(hx, y, hz, core), device_id_type=MESH
+            )
+
+        return 0
+
+    lax.fori_loop(0, 32, greet, 0)
+
+    @pl.when(busy)
+    def _():
+        for there in (
+            device_at(x, up, z, core), device_at(x, down, z, core), device_at(x, y, z, 1 - core),
+        ):
+            pl.semaphore_signal(barrier, inc=1, device_id=there, device_id_type=MESH)
+
     loads = [
         pltpu.make_async_copy(ref, rows_in.at[n], load_sem.at[n])
         for n, ref in enumerate((k_ref, v_ref, q_ref))
@@ -59,28 +84,6 @@
 
     mask_copy = pltpu.make_async_copy(mask_ref, mask, mask_sem)
     mask_copy.start()
-    barrier = pltpu.get_barrier_semaphore()
-
-    def greet(i, _):
-        hx, hz = i // 8, (z + i) % 8
-
-        @pl.when((hx * 8 + hz != me) & (busy | (hx < 3)))
-        def _():
-            pl.semaphore_signal(
-                barrier, inc=1, device_id=device_at(hx, y, hz, core), device_id_type=MESH
-            )
-
-        return 0
-
-    lax.fori_loop(0, 32, greet, 0)
-
-    @pl.when(busy)
-    def _():
-        for there in (
-            device_at(x, up, z, core), device_at(x, down, z, core), device_at(x, y, z, 1 - core),
-        ):
-            pl.semaphore_signal(barrier, inc=1, device_id=there, device_id_type=MESH)
-
     @pl.when(busy)
     def _():
         mask_copy.wait()
@@ -351,7 +354,8 @@
                 total = jnp.sum(totals[rows, :] * gains[rows, :], axis=1, keepdims=True)
                 obuf[rows, :] = (acc[rows, :] / total).astype(jnp.bfloat16)
 
-            def send_back(there, _):
+            def send_back(i, _):
+                there = (i + x * 2 + zl) % 8
                 piece = q_block * 8 + there
                 source = obuf.at[pl.ds(pl.multiple_of(piece * PIECE, PIECE), PIECE), :]
                 target = out_ref.at[:, pl.ds(pl.multiple_of(me * HEAD_DIM, HEAD_DIM), HEAD_DIM)]

time: 47.8 us -> 47.9 us (level)
  no operation moved by 1% of the time
where the time goes in v5:
time: 47.9 us; the launch traced here: 47.8 us
  Pallas kernels  47 us (98%)
  other arithmetic  0.77 us (2%)
    pallas_call x1, Pallas kernels, local(): pl.pallas_call(kernel, out_shape=jax.ShapeDtypeStruct(queries.shape, bf16...  47 us

profile of v5, /device:TPU:64, one launch (start us, length us, event | category | flops | bytes accessed | tf_op | source)
XLA Modules:
  0.0 47.8 jit_solution(11555302253072053501)
XLA Ops:
  0.0 47.0 %shard_map.46 = bf16[32,3072]{1,0:T(8,128)(2,1)S(1)} custom-call(bf16[32,3072]{1,0:T(8,128)(2,1)} %q_ref.1, bf16[32,3072]{1,0:T(8,128)(2,1)} %k_ref.1, bf16[32,3072]{1,0:T(8,128)(2,1)} %v_ref.1, s32[64,64]{1,0:T(8,128)} %mask_ref.1), custom_call_target="tpu_custom_call" | custom-call | tf_op jit(solution)/shard_map/pallas_call | solution.py:409
  47.0 0.8 %convert_element_type.3 = f32[32,3072]{1,0:T(8,128)} convert(bf16[32,3072]{1,0:T(8,128)(2,1)S(1)} %shard_map.46) | non-fusion elementwise | flops 98304 | bytes 589824 | tf_op jit(solution)/shard_map/convert_element_type | solution.py:441
